TPU v7x, 32 devices: a whole 2x2x4 slice. The times are simulated.
32 devices in a mesh: groups: 2 (over y), seq: 4 (over z), head: 2 (over x), inner: 2 (over core).
Axes of the slice: x: 2, y: 2, z: 4, core: 2. Of those that a mesh axis runs over, the one named last changes fastest.
Arguments:
- query_rows: bfloat16 [16, 640, 1024], P(('groups', 'seq'), 'inner', 'head'), parts along dimension 0, may hold values from -100 to 100
- key_rows: bfloat16 [16, 640, 128], P(('groups', 'seq')), parts along dimension 0, may hold values from -5 to 5
- value_rows: bfloat16 [16, 640, 128], P(('groups', 'seq')), parts along dimension 0, may hold values from -6 to 6
- slot_block: int32 [8], replicated, may hold values from 0 to 7, as said below
Outputs:
- attended: bfloat16 [16, 640, 1024], P(('groups', 'seq'), 'inner', 'head'), parts along dimension 0
- log_total: float32 [16, 8, 640], P(('groups', 'seq'), 'head', 'inner'), parts along dimension 0
There are 2 independent parts, one for each index of `groups`. A program takes and returns all parts, laid end to end along the dimension named above; an argument that names none is the same for every part. Nothing has to cross between parts.
Inputs may be any that keep to these rules, and one draw needn't show every extreme that they name: slot_block is a permutation of 0 .. 7; slots 2 s and 2 s + 1 hold blocks b and 7 - b.
All inputs are finite; a program needn't handle non-finite values.
Results may differ from a plain program's by a relative error of at most 0.017.
Values may be sent and summed in bfloat16 or wider, within the bound.
No kernel may reach another device: no remote copies, remote signals or barrier semaphores. Data moves between devices by JAX's collectives and lax.ppermute only.
A program may use at most 64 MiB of HBM per device.

v0:
```python
import math

import jax
import jax.numpy as jnp
from jax import lax
from jax.sharding import PartitionSpec as P


def from_behind(block, axis, distance):
    devices = range(lax.axis_size(axis))
    route = [((i - distance) % len(devices), i) for i in devices]
    return lax.ppermute(block, axis, route)


def shortened(x):
    return jax.tree.map(lambda a: a.astype(jnp.bfloat16) if a.dtype == jnp.float32 else a, x)


def body(query_rows, key_rows, value_rows, slot_block):
    head_width = key_rows.shape[2]
    block_len = key_rows.shape[1]
    row_count = query_rows.shape[1]
    heads_here = query_rows.shape[2] // head_width
    score_scale = 1.0 / math.sqrt(head_width)
    seq_count = lax.axis_size("seq")
    seq_index = lax.axis_index("seq")
    inner_index = lax.axis_index("inner")
    row_iota = jnp.arange(row_count, dtype=jnp.int32)
    col_iota = jnp.arange(block_len, dtype=jnp.int32)

    def query_pos(device):
        held = lax.dynamic_slice_in_dim(slot_block, device * 2, 2)
        return (held[:, None] * block_len + inner_index * row_count + row_iota[None, :]).reshape(-1)

    def attend(running, queries, q_pos, key_block, value_block, k_pos):
        visible = jnp.min(k_pos) <= jnp.max(q_pos)

        def update(state):
            top_run, total_run, accum = state
            scores = (
                jnp.einsum("rhd,cd->hrc", queries, key_block, preferred_element_type=jnp.float32)
                * score_scale
            )
            allowed = k_pos[None, None, :] <= q_pos[None, :, None]
            scores = jnp.where(allowed, scores, -1e30)
            top_new = jnp.maximum(top_run, jnp.max(scores, axis=-1))
            weights = jnp.where(allowed, jnp.exp(scores - top_new[..., None]), 0.0)
            shrink = jnp.exp(top_run - top_new)
            total_new = total_run * shrink + jnp.sum(weights, axis=-1)
            accum_new = accum * shrink[..., None] + jnp.einsum(
                "hrc,cd->hrd",
                weights.astype(jnp.bfloat16),
                value_block,
                preferred_element_type=jnp.float32,
            )
            return (top_new, total_new, accum_new)

        return lax.cond(visible, update, lambda state: state, running)

    local_blocks = lax.dynamic_slice_in_dim(slot_block, seq_index * 2, 2)

    def local_keys(running, queries, q_pos):
        for slot in range(2):
            k_pos = local_blocks[slot] * block_len + col_iota
            running = attend(running, queries, q_pos, key_rows[slot], value_rows[slot], k_pos)
        return running

    empty = (
        jnp.full((heads_here, 2 * row_count), -1e30, jnp.float32),
        jnp.zeros((heads_here, 2 * row_count), jnp.float32),
        jnp.zeros((heads_here, 2 * row_count, head_width), jnp.float32),
    )
    home_queries = query_rows.reshape(2 * row_count, heads_here, head_width)

    def cycle_step(step, carried):
        visiting, running = carried
        anchor = (seq_index - step) % seq_count
        running = local_keys(running, visiting, query_pos(anchor))
        visiting = from_behind(visiting, "seq", 1)
        running = jax.tree.map(
            lambda part, own: part.astype(own.dtype),
            from_behind(shortened(running), "seq", 1),
            running,
        )
        return (visiting, running)

    final_queries, finished = lax.fori_loop(0, seq_count, cycle_step, (home_queries, empty))
    top_run, total_run, accum = finished
    outputs = accum / total_run[..., None]
    attended = (
        jnp.transpose(outputs, (1, 0, 2))
        .reshape(2, row_count, heads_here * head_width)
        .astype(jnp.bfloat16)
    )
    log_total = (top_run + jnp.log(total_run)).reshape(heads_here, 2, row_count)
    log_total = jnp.transpose(log_total, (1, 0, 2))
    return (attended, log_total)


def solution(mesh):
    placed = (
        P(("groups", "seq"), "inner", "head"),
        P(("groups", "seq"), None, None),
        P(("groups", "seq"), None, None),
        P(),
    )
    return jax.shard_map(
        body,
        mesh=mesh,
        in_specs=placed,
        out_specs=(P(("groups", "seq"), "inner", "head"), P(("groups", "seq"), "head", "inner")),
        check_vma=False,
    )
```

profile of v0, /device:TPU:0, one launch (start us, length us, event | category | flops | bytes accessed | tf_op | source)
XLA Modules:
  0.0 207.9 jit_solution(14113934502705064930)
XLA Ops:
  3.3 1.6 reshape.102
  5.0 200.1 %while.23 = (s32[]{:T(128)}, bf16[640,4,128]{2,0,1:T(8,128)(2,1)S(1)}, f32[4,640]{1,0:T(4,128)S(1)}, f32[4,640]{1,0:T(4,128)S(1)}, f32[4,640,128]{2,1,0:T(8,128)...) while((s32[]{:T(128)}, ...), condition=%wide.region_12.13_spmd.clone.clone, body=%wide.region_0.12_spmd.clone.clone.sunk | while | flops 1723463680 | bytes 67346808 | solution.py:87
  9.9 1.7 slice_bitcast_fusion.3
  11.7 5.6 %conditional.8 = ((f32[4,640]{1,0:T(4,128)S(1)}, f32[4,640]{1,0:T(4,128)S(1)}, f32[4,640,128]{2,1,0:T(8,128)S(1)})) conditional(s32[]{:T(128)} %convert_element_type.134, (f32[4,640]{1,0:T(4,128)S(1)}, f32[4,640]{1,0:T(4,128)S(1)}, f32[4,640,128]{2,1,0:T(8,128)S(1)}) %tuple.91, (s32[640]{0:T(1024)S(1)}, s32[2,320]{1,0:T(2,128)S(1)}, ...), branch_computations={%region_4.4_spmd, %region_5.0_spmd} | conditional | flops 861230080 | bytes 25733180 | solution.py:58
  13.4 1.6 fusion.6
  15.0 2.3 %fusion.10 = f32[4,640,128]{2,1,0:T(8,128)S(1)} fusion(f32[640,640,4]{1,0,2:T(8,128)S(1)} %get-tuple-element.528, f32[4,640]{1,0:T(4,128)S(1)} %max.4, pred[640,640]{0,1:T(8,128)(4,1)S(1)} %broadcast_compare_fusion, f32[4,640,128]{2,1,0:T(8,128)S(1)} %get-tuple-element.358, f32[4,640]{1,0:T(4,128)S(1)} %get-tuple-element.524, bf16[640,128]{1,0:T(8,128)(2,1)S(1)} %copy-done.1), kind=kOutput, calls=%fused_computation.9 | convolution fusion | flops 428277760 | bytes 9768960 | tf_op jit(solution)/shard_map/while/body/eval_jaxpr/cond/branch_1_fun/hrc,cd->hrd/dot_general | solution.py:50
  17.4 5.6 %conditional.9 = ((f32[4,640]{1,0:T(4,128)S(1)}, f32[4,640]{1,0:T(4,128)S(1)}, f32[4,640,128]{2,1,0:T(8,128)S(1)})) conditional(s32[]{:T(128)} %convert_element_type.133, (f32[4,640]{1,0:T(4,128)S(1)}, f32[4,640]{1,0:T(4,128)S(1)}, f32[4,640,128]{2,1,0:T(8,128)S(1)}) %get-tuple-element.714, (s32[640]{0:T(1024)S(1)}, s32[2,320]{1,0:T(2,128)S(1)}, ...), branch_computations={%region_8.8_spmd, %region_9.11_spmd} | conditional | flops 861230080 | bytes 25077792 | solution.py:58
  19.1 1.6 fusion.21
  20.7 2.3 %fusion.25 = f32[4,640,128]{2,1,0:T(8,128)S(1)} fusion(f32[640,640,4]{1,0,2:T(8,128)S(1)} %get-tuple-element.530, f32[4,640]{1,0:T(4,128)S(1)} %max.5, pred[640,640]{0,1:T(8,128)(4,1)S(1)} %broadcast_compare_fusion.1, f32[4,640,128]{2,1,0:T(8,128)S(1)} %get-tuple-element.366, f32[4,640]{1,0:T(4,128)S(1)} %get-tuple-element.526, ...), kind=kOutput, calls=%fused_computation.26 | convolution fusion | flops 428277760 | bytes 9768960 | tf_op jit(solution)/shard_map/while/body/eval_jaxpr/cond/branch_1_fun/hrc,cd->hrd/dot_general | solution.py:50
  23.1 3.1 %collective-permute-start.3 = (bf16[4,640,128]{2,1,0:T(8,128)(2,1)S(1)}, bf16[4,640,128]{2,1,0:T(8,128)(2,1)S(1)}, u32[]{:S(2)}, u32[]{:S(2)}) collective-permute-start(bf16[4,640,128]{2,1,0:T(8,128)(2,1)S(1)} %convert_element_type.139), channel_id=1, source_target_pairs={{12,0},{0,4},{4,8},{8,12},{13,1},{1,5},{5,9},{9,13},{14,2},{2,6},{... | collective-permute-start | bytes 1966088 | tf_op jit(solution)/shard_map/while/body/eval_jaxpr/ppermute | solution.py:12
  29.4 27.7 %collective-permute-done.1 = bf16[4,640]{1,0:T(4,128)(2,1)S(1)} collective-permute-done((bf16[4,640]{1,0:T(4,128)(2,1)S(1)}, bf16[4,640]{1,0:T(4,128)(2,1)S(1)}, u32[]{:S(2)}, u32[]{:S(2)}) %collective-permute-start.1) | collective-permute-done | bytes 5152 | tf_op jit(solution)/shard_map/while/body/eval_jaxpr/ppermute | solution.py:12
  62.1 1.7 slice_bitcast_fusion.3
  64.0 5.6 %conditional.8 = ((f32[4,640]{1,0:T(4,128)S(1)}, f32[4,640]{1,0:T(4,128)S(1)}, f32[4,640,128]{2,1,0:T(8,128)S(1)})) conditional(s32[]{:T(128)} %convert_element_type.134, (f32[4,640]{1,0:T(4,128)S(1)}, f32[4,640]{1,0:T(4,128)S(1)}, f32[4,640,128]{2,1,0:T(8,128)S(1)}) %tuple.91, (s32[640]{0:T(1024)S(1)}, s32[2,320]{1,0:T(2,128)S(1)}, ...), branch_computations={%region_4.4_spmd, %region_5.0_spmd} | conditional | flops 861230080 | bytes 25733180 | solution.py:58
  67.3 2.3 %fusion.10 = f32[4,640,128]{2,1,0:T(8,128)S(1)} fusion(f32[640,640,4]{1,0,2:T(8,128)S(1)} %get-tuple-element.528, f32[4,640]{1,0:T(4,128)S(1)} %max.4, pred[640,640]{0,1:T(8,128)(4,1)S(1)} %broadcast_compare_fusion, f32[4,640,128]{2,1,0:T(8,128)S(1)} %get-tuple-element.358, f32[4,640]{1,0:T(4,128)S(1)} %get-tuple-element.524, bf16[640,128]{1,0:T(8,128)(2,1)S(1)} %copy-done.1), kind=kOutput, calls=%fused_computation.9 | convolution fusion | flops 428277760 | bytes 9768960 | tf_op jit(solution)/shard_map/while/body/eval_jaxpr/cond/branch_1_fun/hrc,cd->hrd/dot_general | solution.py:50
  69.6 5.6 %conditional.9 = ((f32[4,640]{1,0:T(4,128)S(1)}, f32[4,640]{1,0:T(4,128)S(1)}, f32[4,640,128]{2,1,0:T(8,128)S(1)})) conditional(s32[]{:T(128)} %convert_element_type.133, (f32[4,640]{1,0:T(4,128)S(1)}, f32[4,640]{1,0:T(4,128)S(1)}, f32[4,640,128]{2,1,0:T(8,128)S(1)}) %get-tuple-element.714, (s32[640]{0:T(1024)S(1)}, s32[2,320]{1,0:T(2,128)S(1)}, ...), branch_computations={%region_8.8_spmd, %region_9.11_spmd} | conditional | flops 861230080 | bytes 25077792 | solution.py:58
  73.0 2.3 %fusion.25 = f32[4,640,128]{2,1,0:T(8,128)S(1)} fusion(f32[640,640,4]{1,0,2:T(8,128)S(1)} %get-tuple-element.530, f32[4,640]{1,0:T(4,128)S(1)} %max.5, pred[640,640]{0,1:T(8,128)(4,1)S(1)} %broadcast_compare_fusion.1, f32[4,640,128]{2,1,0:T(8,128)S(1)} %get-tuple-element.366, f32[4,640]{1,0:T(4,128)S(1)} %get-tuple-element.526, ...), kind=kOutput, calls=%fused_computation.26 | convolution fusion | flops 428277760 | bytes 9768960 | tf_op jit(solution)/shard_map/while/body/eval_jaxpr/cond/branch_1_fun/hrc,cd->hrd/dot_general | solution.py:50
  78.3 2.1 %collective-permute-start.2 = (bf16[4,640]{1,0:T(4,128)(2,1)S(1)}, bf16[4,640]{1,0:T(4,128)(2,1)S(1)}, u32[]{:S(2)}, u32[]{:S(2)}) collective-permute-start(bf16[4,640]{1,0:T(4,128)(2,1)S(1)} %convert_element_type.137), channel_id=1, source_target_pairs={{12,0},{0,4},{4,8},{8,12},{13,1},{1,5},{5,9},{9,13},{14,2},{2,6},{... | collective-permute-start | bytes 15368 | tf_op jit(solution)/shard_map/while/body/eval_jaxpr/ppermute | solution.py:12
  80.4 27.0 %collective-permute-done.1 = bf16[4,640]{1,0:T(4,128)(2,1)S(1)} collective-permute-done((bf16[4,640]{1,0:T(4,128)(2,1)S(1)}, bf16[4,640]{1,0:T(4,128)(2,1)S(1)}, u32[]{:S(2)}, u32[]{:S(2)}) %collective-permute-start.1) | collective-permute-done | bytes 5152 | tf_op jit(solution)/shard_map/while/body/eval_jaxpr/ppermute | solution.py:12
  112.3 1.7 slice_bitcast_fusion.3
  114.2 5.6 %conditional.8 = ((f32[4,640]{1,0:T(4,128)S(1)}, f32[4,640]{1,0:T(4,128)S(1)}, f32[4,640,128]{2,1,0:T(8,128)S(1)})) conditional(s32[]{:T(128)} %convert_element_type.134, (f32[4,640]{1,0:T(4,128)S(1)}, f32[4,640]{1,0:T(4,128)S(1)}, f32[4,640,128]{2,1,0:T(8,128)S(1)}) %tuple.91, (s32[640]{0:T(1024)S(1)}, s32[2,320]{1,0:T(2,128)S(1)}, ...), branch_computations={%region_4.4_spmd, %region_5.0_spmd} | conditional | flops 861230080 | bytes 25733180 | solution.py:58
  117.5 2.3 %fusion.10 = f32[4,640,128]{2,1,0:T(8,128)S(1)} fusion(f32[640,640,4]{1,0,2:T(8,128)S(1)} %get-tuple-element.528, f32[4,640]{1,0:T(4,128)S(1)} %max.4, pred[640,640]{0,1:T(8,128)(4,1)S(1)} %broadcast_compare_fusion, f32[4,640,128]{2,1,0:T(8,128)S(1)} %get-tuple-element.358, f32[4,640]{1,0:T(4,128)S(1)} %get-tuple-element.524, bf16[640,128]{1,0:T(8,128)(2,1)S(1)} %copy-done.1), kind=kOutput, calls=%fused_computation.9 | convolution fusion | flops 428277760 | bytes 9768960 | tf_op jit(solution)/shard_map/while/body/eval_jaxpr/cond/branch_1_fun/hrc,cd->hrd/dot_general | solution.py:50
  119.8 5.6 %conditional.9 = ((f32[4,640]{1,0:T(4,128)S(1)}, f32[4,640]{1,0:T(4,128)S(1)}, f32[4,640,128]{2,1,0:T(8,128)S(1)})) conditional(s32[]{:T(128)} %convert_element_type.133, (f32[4,640]{1,0:T(4,128)S(1)}, f32[4,640]{1,0:T(4,128)S(1)}, f32[4,640,128]{2,1,0:T(8,128)S(1)}) %get-tuple-element.714, (s32[640]{0:T(1024)S(1)}, s32[2,320]{1,0:T(2,128)S(1)}, ...), branch_computations={%region_8.8_spmd, %region_9.11_spmd} | conditional | flops 861230080 | bytes 25077792 | solution.py:58
  123.2 2.3 %fusion.25 = f32[4,640,128]{2,1,0:T(8,128)S(1)} fusion(f32[640,640,4]{1,0,2:T(8,128)S(1)} %get-tuple-element.530, f32[4,640]{1,0:T(4,128)S(1)} %max.5, pred[640,640]{0,1:T(8,128)(4,1)S(1)} %broadcast_compare_fusion.1, f32[4,640,128]{2,1,0:T(8,128)S(1)} %get-tuple-element.366, f32[4,640]{1,0:T(4,128)S(1)} %get-tuple-element.526, ...), kind=kOutput, calls=%fused_computation.26 | convolution fusion | flops 428277760 | bytes 9768960 | tf_op jit(solution)/shard_map/while/body/eval_jaxpr/cond/branch_1_fun/hrc,cd->hrd/dot_general | solution.py:50
  126.4 4.2 %collective-permute-start.2 = (bf16[4,640]{1,0:T(4,128)(2,1)S(1)}, bf16[4,640]{1,0:T(4,128)(2,1)S(1)}, u32[]{:S(2)}, u32[]{:S(2)}) collective-permute-start(bf16[4,640]{1,0:T(4,128)(2,1)S(1)} %convert_element_type.137), channel_id=1, source_target_pairs={{12,0},{0,4},{4,8},{8,12},{13,1},{1,5},{5,9},{9,13},{14,2},{2,6},{... | collective-permute-start | bytes 15368 | tf_op jit(solution)/shard_map/while/body/eval_jaxpr/ppermute | solution.py:12
  130.6 26.0 %collective-permute-done.1 = bf16[4,640]{1,0:T(4,128)(2,1)S(1)} collective-permute-done((bf16[4,640]{1,0:T(4,128)(2,1)S(1)}, bf16[4,640]{1,0:T(4,128)(2,1)S(1)}, u32[]{:S(2)}, u32[]{:S(2)}) %collective-permute-start.1) | collective-permute-done | bytes 5152 | tf_op jit(solution)/shard_map/while/body/eval_jaxpr/ppermute | solution.py:12
  161.6 1.7 slice_bitcast_fusion.3
  163.5 5.6 %conditional.8 = ((f32[4,640]{1,0:T(4,128)S(1)}, f32[4,640]{1,0:T(4,128)S(1)}, f32[4,640,128]{2,1,0:T(8,128)S(1)})) conditional(s32[]{:T(128)} %convert_element_type.134, (f32[4,640]{1,0:T(4,128)S(1)}, f32[4,640]{1,0:T(4,128)S(1)}, f32[4,640,128]{2,1,0:T(8,128)S(1)}) %tuple.91, (s32[640]{0:T(1024)S(1)}, s32[2,320]{1,0:T(2,128)S(1)}, ...), branch_computations={%region_4.4_spmd, %region_5.0_spmd} | conditional | flops 861230080 | bytes 25733180 | solution.py:58
  166.8 2.3 %fusion.10 = f32[4,640,128]{2,1,0:T(8,128)S(1)} fusion(f32[640,640,4]{1,0,2:T(8,128)S(1)} %get-tuple-element.528, f32[4,640]{1,0:T(4,128)S(1)} %max.4, pred[640,640]{0,1:T(8,128)(4,1)S(1)} %broadcast_compare_fusion, f32[4,640,128]{2,1,0:T(8,128)S(1)} %get-tuple-element.358, f32[4,640]{1,0:T(4,128)S(1)} %get-tuple-element.524, bf16[640,128]{1,0:T(8,128)(2,1)S(1)} %copy-done.1), kind=kOutput, calls=%fused_computation.9 | convolution fusion | flops 428277760 | bytes 9768960 | tf_op jit(solution)/shard_map/while/body/eval_jaxpr/cond/branch_1_fun/hrc,cd->hrd/dot_general | solution.py:50
  169.1 5.6 %conditional.9 = ((f32[4,640]{1,0:T(4,128)S(1)}, f32[4,640]{1,0:T(4,128)S(1)}, f32[4,640,128]{2,1,0:T(8,128)S(1)})) conditional(s32[]{:T(128)} %convert_element_type.133, (f32[4,640]{1,0:T(4,128)S(1)}, f32[4,640]{1,0:T(4,128)S(1)}, f32[4,640,128]{2,1,0:T(8,128)S(1)}) %get-tuple-element.714, (s32[640]{0:T(1024)S(1)}, s32[2,320]{1,0:T(2,128)S(1)}, ...), branch_computations={%region_8.8_spmd, %region_9.11_spmd} | conditional | flops 861230080 | bytes 25077792 | solution.py:58
  172.5 2.3 %fusion.25 = f32[4,640,128]{2,1,0:T(8,128)S(1)} fusion(f32[640,640,4]{1,0,2:T(8,128)S(1)} %get-tuple-element.530, f32[4,640]{1,0:T(4,128)S(1)} %max.5, pred[640,640]{0,1:T(8,128)(4,1)S(1)} %broadcast_compare_fusion.1, f32[4,640,128]{2,1,0:T(8,128)S(1)} %get-tuple-element.366, f32[4,640]{1,0:T(4,128)S(1)} %get-tuple-element.526, ...), kind=kOutput, calls=%fused_computation.26 | convolution fusion | flops 428277760 | bytes 9768960 | tf_op jit(solution)/shard_map/while/body/eval_jaxpr/cond/branch_1_fun/hrc,cd->hrd/dot_general | solution.py:50
  175.1 4.8 %collective-permute-start.2 = (bf16[4,640]{1,0:T(4,128)(2,1)S(1)}, bf16[4,640]{1,0:T(4,128)(2,1)S(1)}, u32[]{:S(2)}, u32[]{:S(2)}) collective-permute-start(bf16[4,640]{1,0:T(4,128)(2,1)S(1)} %convert_element_type.137), channel_id=1, source_target_pairs={{12,0},{0,4},{4,8},{8,12},{13,1},{1,5},{5,9},{9,13},{14,2},{2,6},{... | collective-permute-start | bytes 15368 | tf_op jit(solution)/shard_map/while/body/eval_jaxpr/ppermute | solution.py:12
  179.9 25.1 %collective-permute-done.1 = bf16[4,640]{1,0:T(4,128)(2,1)S(1)} collective-permute-done((bf16[4,640]{1,0:T(4,128)(2,1)S(1)}, bf16[4,640]{1,0:T(4,128)(2,1)S(1)}, u32[]{:S(2)}, u32[]{:S(2)}) %collective-permute-start.1) | collective-permute-done | bytes 5152 | tf_op jit(solution)/shard_map/while/body/eval_jaxpr/ppermute | solution.py:12
  (166 shorter events, 44.6 us)
Async XLA Ops:
  11.7 5.7 %copy-start = (bf16[2,640,128]{2,1,0:T(8,128)(2,1)S(1)}, bf16[2,640,128]{2,1,0:T(8,128)(2,1)}, u32[]{:S(2)}) copy-start(bf16[2,640,128]{2,1,0:T(8,128)(2,1)} %get-tuple-element.706) | copy-start | bytes 983044 | tf_op jit(solution)/shard_map/while
  11.7 5.7 %copy-start.2 = (bf16[2,640,128]{2,1,0:T(8,128)(2,1)S(1)}, bf16[2,640,128]{2,1,0:T(8,128)(2,1)}, u32[]{:S(2)}) copy-start(bf16[2,640,128]{2,1,0:T(8,128)(2,1)} %get-tuple-element.707) | copy-start | bytes 983044 | tf_op jit(solution)/shard_map/while
  12.1 2.9 %copy-start.1 = (bf16[640,128]{1,0:T(8,128)(2,1)S(1)}, bf16[640,128]{1,0:T(8,128)(2,1)}, u32[]{:S(2)}) copy-start(bf16[640,128]{1,0:T(8,128)(2,1)} %get-tuple-element.359) | copy-start | bytes 491524 | tf_op jit(solution)/shard_map/while/body/eval_jaxpr/cond
  23.1 34.1 %collective-permute-start.3 = (bf16[4,640,128]{2,1,0:T(8,128)(2,1)S(1)}, bf16[4,640,128]{2,1,0:T(8,128)(2,1)S(1)}, u32[]{:S(2)}, u32[]{:S(2)}) collective-permute-start(bf16[4,640,128]{2,1,0:T(8,128)(2,1)S(1)} %convert_element_type.139), channel_id=1, source_target_pairs={{12,0},{0,4},{4,8},{8,12},{13,1},{1,5},{5,9},{9,13},{14,2},{2,6},{... | collective-permute-start | bytes 1966088 | tf_op jit(solution)/shard_map/while/body/eval_jaxpr/ppermute | solution.py:12
  26.2 31.1 %collective-permute-start = (bf16[640,4,128]{2,0,1:T(8,128)(2,1)S(1)}, bf16[640,4,128]{2,0,1:T(8,128)(2,1)S(1)}, u32[]{:S(2)}, u32[]{:S(2)}) collective-permute-start(bf16[640,4,128]{2,0,1:T(8,128)(2,1)S(1)} %copy.34), channel_id=1, source_target_pairs={{12,0},{0,4},{4,8},{8,12},{13,1},{1,5},{5,9},{9,13},{14,2},{2,6},{... | collective-permute-start | bytes 1966088 | tf_op jit(solution)/shard_map/while/body/eval_jaxpr/ppermute | solution.py:12
  27.7 29.4 %collective-permute-start.1 = (bf16[4,640]{1,0:T(4,128)(2,1)S(1)}, bf16[4,640]{1,0:T(4,128)(2,1)S(1)}, u32[]{:S(2)}, u32[]{:S(2)}) collective-permute-start(bf16[4,640]{1,0:T(4,128)(2,1)S(1)} %convert_element_type.135), channel_id=1, source_target_pairs={{12,0},{0,4},{4,8},{8,12},{13,1},{1,5},{5,9},{9,13},{14,2},{2,6},{... | collective-permute-start | bytes 15368 | tf_op jit(solution)/shard_map/while/body/eval_jaxpr/ppermute | solution.py:12
  29.3 27.9 %collective-permute-start.2 = (bf16[4,640]{1,0:T(4,128)(2,1)S(1)}, bf16[4,640]{1,0:T(4,128)(2,1)S(1)}, u32[]{:S(2)}, u32[]{:S(2)}) collective-permute-start(bf16[4,640]{1,0:T(4,128)(2,1)S(1)} %convert_element_type.137), channel_id=1, source_target_pairs={{12,0},{0,4},{4,8},{8,12},{13,1},{1,5},{5,9},{9,13},{14,2},{2,6},{... | collective-permute-start | bytes 15368 | tf_op jit(solution)/shard_map/while/body/eval_jaxpr/ppermute | solution.py:12
  63.9 5.7 %copy-start = (bf16[2,640,128]{2,1,0:T(8,128)(2,1)S(1)}, bf16[2,640,128]{2,1,0:T(8,128)(2,1)}, u32[]{:S(2)}) copy-start(bf16[2,640,128]{2,1,0:T(8,128)(2,1)} %get-tuple-element.706) | copy-start | bytes 983044 | tf_op jit(solution)/shard_map/while
  63.9 5.7 %copy-start.2 = (bf16[2,640,128]{2,1,0:T(8,128)(2,1)S(1)}, bf16[2,640,128]{2,1,0:T(8,128)(2,1)}, u32[]{:S(2)}) copy-start(bf16[2,640,128]{2,1,0:T(8,128)(2,1)} %get-tuple-element.707) | copy-start | bytes 983044 | tf_op jit(solution)/shard_map/while
  64.4 2.9 %copy-start.1 = (bf16[640,128]{1,0:T(8,128)(2,1)S(1)}, bf16[640,128]{1,0:T(8,128)(2,1)}, u32[]{:S(2)}) copy-start(bf16[640,128]{1,0:T(8,128)(2,1)} %get-tuple-element.359) | copy-start | bytes 491524 | tf_op jit(solution)/shard_map/while/body/eval_jaxpr/cond
  75.4 32.0 %collective-permute-start.3 = (bf16[4,640,128]{2,1,0:T(8,128)(2,1)S(1)}, bf16[4,640,128]{2,1,0:T(8,128)(2,1)S(1)}, u32[]{:S(2)}, u32[]{:S(2)}) collective-permute-start(bf16[4,640,128]{2,1,0:T(8,128)(2,1)S(1)} %convert_element_type.139), channel_id=1, source_target_pairs={{12,0},{0,4},{4,8},{8,12},{13,1},{1,5},{5,9},{9,13},{14,2},{2,6},{... | collective-permute-start | bytes 1966088 | tf_op jit(solution)/shard_map/while/body/eval_jaxpr/ppermute | solution.py:12
  75.4 32.1 %collective-permute-start = (bf16[640,4,128]{2,0,1:T(8,128)(2,1)S(1)}, bf16[640,4,128]{2,0,1:T(8,128)(2,1)S(1)}, u32[]{:S(2)}, u32[]{:S(2)}) collective-permute-start(bf16[640,4,128]{2,0,1:T(8,128)(2,1)S(1)} %copy.34), channel_id=1, source_target_pairs={{12,0},{0,4},{4,8},{8,12},{13,1},{1,5},{5,9},{9,13},{14,2},{2,6},{... | collective-permute-start | bytes 1966088 | tf_op jit(solution)/shard_map/while/body/eval_jaxpr/ppermute | solution.py:12
  76.7 30.6 %collective-permute-start.1 = (bf16[4,640]{1,0:T(4,128)(2,1)S(1)}, bf16[4,640]{1,0:T(4,128)(2,1)S(1)}, u32[]{:S(2)}, u32[]{:S(2)}) collective-permute-start(bf16[4,640]{1,0:T(4,128)(2,1)S(1)} %convert_element_type.135), channel_id=1, source_target_pairs={{12,0},{0,4},{4,8},{8,12},{13,1},{1,5},{5,9},{9,13},{14,2},{2,6},{... | collective-permute-start | bytes 15368 | tf_op jit(solution)/shard_map/while/body/eval_jaxpr/ppermute | solution.py:12
  78.3 29.1 %collective-permute-start.2 = (bf16[4,640]{1,0:T(4,128)(2,1)S(1)}, bf16[4,640]{1,0:T(4,128)(2,1)S(1)}, u32[]{:S(2)}, u32[]{:S(2)}) collective-permute-start(bf16[4,640]{1,0:T(4,128)(2,1)S(1)} %convert_element_type.137), channel_id=1, source_target_pairs={{12,0},{0,4},{4,8},{8,12},{13,1},{1,5},{5,9},{9,13},{14,2},{2,6},{... | collective-permute-start | bytes 15368 | tf_op jit(solution)/shard_map/while/body/eval_jaxpr/ppermute | solution.py:12
  114.1 5.7 %copy-start = (bf16[2,640,128]{2,1,0:T(8,128)(2,1)S(1)}, bf16[2,640,128]{2,1,0:T(8,128)(2,1)}, u32[]{:S(2)}) copy-start(bf16[2,640,128]{2,1,0:T(8,128)(2,1)} %get-tuple-element.706) | copy-start | bytes 983044 | tf_op jit(solution)/shard_map/while
  114.2 5.7 %copy-start.2 = (bf16[2,640,128]{2,1,0:T(8,128)(2,1)S(1)}, bf16[2,640,128]{2,1,0:T(8,128)(2,1)}, u32[]{:S(2)}) copy-start(bf16[2,640,128]{2,1,0:T(8,128)(2,1)} %get-tuple-element.707) | copy-start | bytes 983044 | tf_op jit(solution)/shard_map/while
  114.6 2.9 %copy-start.1 = (bf16[640,128]{1,0:T(8,128)(2,1)S(1)}, bf16[640,128]{1,0:T(8,128)(2,1)}, u32[]{:S(2)}) copy-start(bf16[640,128]{1,0:T(8,128)(2,1)} %get-tuple-element.359) | copy-start | bytes 491524 | tf_op jit(solution)/shard_map/while/body/eval_jaxpr/cond
  125.6 31.1 %collective-permute-start.3 = (bf16[4,640,128]{2,1,0:T(8,128)(2,1)S(1)}, bf16[4,640,128]{2,1,0:T(8,128)(2,1)S(1)}, u32[]{:S(2)}, u32[]{:S(2)}) collective-permute-start(bf16[4,640,128]{2,1,0:T(8,128)(2,1)S(1)} %convert_element_type.139), channel_id=1, source_target_pairs={{12,0},{0,4},{4,8},{8,12},{13,1},{1,5},{5,9},{9,13},{14,2},{2,6},{... | collective-permute-start | bytes 1966088 | tf_op jit(solution)/shard_map/while/body/eval_jaxpr/ppermute | solution.py:12
  125.6 31.2 %collective-permute-start = (bf16[640,4,128]{2,0,1:T(8,128)(2,1)S(1)}, bf16[640,4,128]{2,0,1:T(8,128)(2,1)S(1)}, u32[]{:S(2)}, u32[]{:S(2)}) collective-permute-start(bf16[640,4,128]{2,0,1:T(8,128)(2,1)S(1)} %copy.34), channel_id=1, source_target_pairs={{12,0},{0,4},{4,8},{8,12},{13,1},{1,5},{5,9},{9,13},{14,2},{2,6},{... | collective-permute-start | bytes 1966088 | tf_op jit(solution)/shard_map/while/body/eval_jaxpr/ppermute | solution.py:12
  125.7 30.9 %collective-permute-start.1 = (bf16[4,640]{1,0:T(4,128)(2,1)S(1)}, bf16[4,640]{1,0:T(4,128)(2,1)S(1)}, u32[]{:S(2)}, u32[]{:S(2)}) collective-permute-start(bf16[4,640]{1,0:T(4,128)(2,1)S(1)} %convert_element_type.135), channel_id=1, source_target_pairs={{12,0},{0,4},{4,8},{8,12},{13,1},{1,5},{5,9},{9,13},{14,2},{2,6},{... | collective-permute-start | bytes 15368 | tf_op jit(solution)/shard_map/while/body/eval_jaxpr/ppermute | solution.py:12
  126.4 30.3 %collective-permute-start.2 = (bf16[4,640]{1,0:T(4,128)(2,1)S(1)}, bf16[4,640]{1,0:T(4,128)(2,1)S(1)}, u32[]{:S(2)}, u32[]{:S(2)}) collective-permute-start(bf16[4,640]{1,0:T(4,128)(2,1)S(1)} %convert_element_type.137), channel_id=1, source_target_pairs={{12,0},{0,4},{4,8},{8,12},{13,1},{1,5},{5,9},{9,13},{14,2},{2,6},{... | collective-permute-start | bytes 15368 | tf_op jit(solution)/shard_map/while/body/eval_jaxpr/ppermute | solution.py:12
  163.4 5.7 %copy-start = (bf16[2,640,128]{2,1,0:T(8,128)(2,1)S(1)}, bf16[2,640,128]{2,1,0:T(8,128)(2,1)}, u32[]{:S(2)}) copy-start(bf16[2,640,128]{2,1,0:T(8,128)(2,1)} %get-tuple-element.706) | copy-start | bytes 983044 | tf_op jit(solution)/shard_map/while
  163.4 5.7 %copy-start.2 = (bf16[2,640,128]{2,1,0:T(8,128)(2,1)S(1)}, bf16[2,640,128]{2,1,0:T(8,128)(2,1)}, u32[]{:S(2)}) copy-start(bf16[2,640,128]{2,1,0:T(8,128)(2,1)} %get-tuple-element.707) | copy-start | bytes 983044 | tf_op jit(solution)/shard_map/while
  163.9 2.9 %copy-start.1 = (bf16[640,128]{1,0:T(8,128)(2,1)S(1)}, bf16[640,128]{1,0:T(8,128)(2,1)}, u32[]{:S(2)}) copy-start(bf16[640,128]{1,0:T(8,128)(2,1)} %get-tuple-element.359) | copy-start | bytes 491524 | tf_op jit(solution)/shard_map/while/body/eval_jaxpr/cond
  174.9 30.2 %collective-permute-start.3 = (bf16[4,640,128]{2,1,0:T(8,128)(2,1)S(1)}, bf16[4,640,128]{2,1,0:T(8,128)(2,1)S(1)}, u32[]{:S(2)}, u32[]{:S(2)}) collective-permute-start(bf16[4,640,128]{2,1,0:T(8,128)(2,1)S(1)} %convert_element_type.139), channel_id=1, source_target_pairs={{12,0},{0,4},{4,8},{8,12},{13,1},{1,5},{5,9},{9,13},{14,2},{2,6},{... | collective-permute-start | bytes 1966088 | tf_op jit(solution)/shard_map/while/body/eval_jaxpr/ppermute | solution.py:12
  174.9 30.2 %collective-permute-start = (bf16[640,4,128]{2,0,1:T(8,128)(2,1)S(1)}, bf16[640,4,128]{2,0,1:T(8,128)(2,1)S(1)}, u32[]{:S(2)}, u32[]{:S(2)}) collective-permute-start(bf16[640,4,128]{2,0,1:T(8,128)(2,1)S(1)} %copy.34), channel_id=1, source_target_pairs={{12,0},{0,4},{4,8},{8,12},{13,1},{1,5},{5,9},{9,13},{14,2},{2,6},{... | collective-permute-start | bytes 1966088 | tf_op jit(solution)/shard_map/while/body/eval_jaxpr/ppermute | solution.py:12
  175.0 30.0 %collective-permute-start.1 = (bf16[4,640]{1,0:T(4,128)(2,1)S(1)}, bf16[4,640]{1,0:T(4,128)(2,1)S(1)}, u32[]{:S(2)}, u32[]{:S(2)}) collective-permute-start(bf16[4,640]{1,0:T(4,128)(2,1)S(1)} %convert_element_type.135), channel_id=1, source_target_pairs={{12,0},{0,4},{4,8},{8,12},{13,1},{1,5},{5,9},{9,13},{14,2},{2,6},{... | collective-permute-start | bytes 15368 | tf_op jit(solution)/shard_map/while/body/eval_jaxpr/ppermute | solution.py:12
  175.1 30.0 %collective-permute-start.2 = (bf16[4,640]{1,0:T(4,128)(2,1)S(1)}, bf16[4,640]{1,0:T(4,128)(2,1)S(1)}, u32[]{:S(2)}, u32[]{:S(2)}) collective-permute-start(bf16[4,640]{1,0:T(4,128)(2,1)S(1)} %convert_element_type.137), channel_id=1, source_target_pairs={{12,0},{0,4},{4,8},{8,12},{13,1},{1,5},{5,9},{9,13},{14,2},{2,6},{... | collective-permute-start | bytes 15368 | tf_op jit(solution)/shard_map/while/body/eval_jaxpr/ppermute | solution.py:12
where the time goes:
time: 206 us; the launch traced here: 208 us
  waiting for transfers between devices  106 us (51%)
  matrix products  28.5 us (14%)
  other arithmetic  25.7 us (12%)
  starting transfers between devices  21.2 us (10%)
  local copies, waits for them, and re-layouts  13 us (6%)
  loops' own time  11.4 us (6%)
    ppermute x16, waiting for transfers between devices, from_behind(): return lax.ppermute(block, axis, route)  106 us
    ppermute x16, starting transfers between devices, from_behind(): return lax.ppermute(block, axis, route)  21.2 us
    dot_general x8, matrix products, update(): jnp.einsum('hrc,cd->hrd', weights.astype(jnp.bfloat16), value_block, pref...  18.2 us
    reduce_sum x8, other arithmetic, update(): total_new = total_run * shrink + jnp.sum(weights, axis=-1)  12.9 us
    another operation x1, loops' own time, body(): lax.fori_loop(0, seq_count, cycle_step, (home_queries, empty))  11 us
    dot_general x8, matrix products, update(): jnp.einsum('rhd,cd->hrc', queries, key_block, preferred_element_type=jnp....  10.3 us
    squeeze x4, local copies, waits for them, and re-layouts, local_keys(): value_rows[slot]  6.74 us
    add x8, other arithmetic, query_pos(): held[:, None] * block_len + inner_index * row_count + row_iota[None, :]  6.05 us
  transfers between devices with their start and end apart: 16, of which 4 were waited for; matrix products, arithmetic and copies ran while one was open for 0% of the time, Pallas kernels for 0%

commit v1 on v0

v1 whole, which is shorter than its diff:
```python
import functools
import math

import jax
import jax.numpy as jnp
from jax import lax
from jax.experimental import pallas as pl
from jax.experimental.pallas import tpu as pltpu
from jax.sharding import PartitionSpec as P

NEG = -1e30
SUM_LIMIT = 1e36


def score_dot(q, k):
    return lax.dot_general(q, k, (((1,), (1,)), ((), ())), preferred_element_type=jnp.float32)


def widen(x, width):
    return jnp.concatenate([x] * (width // x.shape[1]), axis=1)


def with_ones(v):
    return jnp.concatenate([v, jnp.ones_like(v)], axis=1)


def local_kernel(coef, sb, q_ref, k_ref, v_ref, acc_ref, top_ref):
    rows, block_len = q_ref.shape[1], k_ref.shape[1]
    me = lax.axis_index("seq")
    inner = lax.axis_index("inner")
    b0, b1 = sb[2 * me], sb[2 * me + 1]
    hi = jnp.where(b1 > b0, 1, 0)
    lo = 1 - hi
    row = lax.broadcasted_iota(jnp.int32, (rows, block_len), 0) + inner * rows
    col = lax.broadcasted_iota(jnp.int32, (rows, block_len), 1)
    causal = col <= row

    def lanes_max(s):
        top = jnp.max(s, axis=1, keepdims=True)
        return jnp.broadcast_to(top, (rows, 128))

    s_diag = jnp.where(causal, score_dot(q_ref[hi], k_ref[hi]) * coef, NEG)
    s_past = score_dot(q_ref[hi], k_ref[lo]) * coef
    s_low = jnp.where(causal, score_dot(q_ref[lo], k_ref[lo]) * coef, NEG)
    top = lanes_max(jnp.maximum(s_diag, s_past))
    wide = widen(top, block_len)
    p_diag = jnp.exp2(s_diag - wide).astype(jnp.bfloat16)
    p_past = jnp.exp2(s_past - wide).astype(jnp.bfloat16)
    v_hi, v_lo = with_ones(v_ref[hi]), with_ones(v_ref[lo])
    acc = jnp.dot(p_diag, v_hi, preferred_element_type=jnp.float32)
    acc += jnp.dot(p_past, v_lo, preferred_element_type=jnp.float32)
    top_ref[hi, 0] = top
    acc_ref[hi, 0] = acc
    top = lanes_max(s_low)
    p_low = jnp.exp2(s_low - widen(top, block_len)).astype(jnp.bfloat16)
    top_ref[lo, 0] = top
    acc_ref[lo, 0] = jnp.dot(p_low, v_lo, preferred_element_type=jnp.float32)


def remote_kernel(coef, count, sb, q_ref, acc_in, top_ref, kv_hbm, out_ref, lse_ref, k_buf, v_buf, acc, run_top, sems):
    rows, block_len = q_ref.shape[1], k_buf.shape[2]
    head = pl.program_id(0)
    me = lax.axis_index("seq")
    inner = lax.axis_index("inner")
    b0, b1 = sb[2 * me], sb[2 * me + 1]
    hi = jnp.where(b1 > b0, 1, 0)
    lo = 1 - hi

    def copies(step):
        source = lax.rem(me + step, count)
        found = []
        for slot in range(2):
            piece = source * 4 + slot * 2
            found.append(
                pltpu.make_async_copy(kv_hbm.at[piece], k_buf.at[step, slot], sems.at[step, slot, 0])
            )
            found.append(
                pltpu.make_async_copy(
                    kv_hbm.at[piece + 1], v_buf.at[step, slot, :, pl.ds(0, 128)], sems.at[step, slot, 1]
                )
            )
        return found

    order = list(range(1, count)) + [0]

    @pl.when(head == 0)
    def _():
        for step in order:
            for copy in copies(step):
                copy.start()
        v_buf[:, :, :, 128:] = jnp.ones((count, 2, block_len, 128), jnp.bfloat16)
        for step in order:
            for copy in copies(step):
                copy.wait()

    acc[...] = acc_in[:, 0]

    def weights(slot, keys):
        s = score_dot(q_ref[slot], keys) * coef
        return jnp.exp2(s - widen(top_ref[slot, 0], block_len)).astype(jnp.bfloat16)

    total = None
    for step in range(1, count):
        source = lax.rem(me + step, count)
        c0, c1 = sb[2 * source], sb[2 * source + 1]
        other_hi = jnp.where(c1 > c0, 1, 0)
        other_lo = 1 - other_hi
        above = jnp.maximum(b0, b1) > jnp.maximum(c0, c1)
        q_slot = jnp.where(above, hi, lo)
        k_slot = jnp.where(above, other_hi, other_lo)
        part = jnp.dot(
            weights(hi, k_buf[step, other_lo]), v_buf[step, other_lo], preferred_element_type=jnp.float32
        )
        total = part if total is None else total + part
        acc[q_slot] += jnp.dot(
            weights(q_slot, k_buf[step, k_slot]), v_buf[step, k_slot], preferred_element_type=jnp.float32
        )
    acc[hi] += total

    largest = jnp.max(acc[:, :, 128:])

    @pl.when(largest < SUM_LIMIT)
    def _():
        run_top[...] = top_ref[:, 0]

    @pl.when(jnp.logical_not(largest < SUM_LIMIT))
    def _():
        run_top[...] = jnp.full_like(run_top, NEG)
        acc[...] = jnp.zeros_like(acc)

        @pl.loop(0, count * 4)
        def _(i):
            step, slot, q_slot = i // 4, lax.rem(i, 4) // 2, lax.rem(i, 2)
            source = lax.rem(me + step, count)
            shift = (sb[2 * me + q_slot] - sb[2 * source + slot]) * block_len + inner * rows

            @pl.when(shift + rows > 0)
            def _():
                s = score_dot(q_ref[q_slot], k_buf[step, slot]) * coef
                row = lax.broadcasted_iota(jnp.int32, s.shape, 0) + shift
                allowed = lax.broadcasted_iota(jnp.int32, s.shape, 1) <= row
                s = jnp.where(allowed, s, NEG)
                before = run_top[q_slot]
                top = jnp.maximum(before, jnp.broadcast_to(jnp.max(s, axis=1, keepdims=True), before.shape))
                p = jnp.where(allowed, jnp.exp2(s - widen(top, block_len)), 0.0).astype(jnp.bfloat16)
                run_top[q_slot] = top
                acc[q_slot] = acc[q_slot] * widen(jnp.exp2(before - top), 256) + jnp.dot(
                    p, v_buf[step, slot], preferred_element_type=jnp.float32
                )

    for slot in range(2):
        sums = acc[slot, :, 128:]
        out_ref[slot] = (acc[slot, :, :128] / sums).astype(out_ref.dtype)
        log_total = run_top[slot] * math.log(2.0) + jnp.log(sums)
        lse_ref[slot, pl.ds(head, 1), :] = jnp.transpose(log_total)[:1]


def body(query_rows, key_rows, value_rows, slot_block):
    _, block_len, width = key_rows.shape
    _, rows, feats = query_rows.shape
    heads = feats // width
    count = lax.axis_size("seq")
    coef = math.log2(math.e) / math.sqrt(width)

    head_index, inner_index = lax.axis_index("head"), lax.axis_index("inner")
    with jax.named_scope("pieces"):
        kv = jnp.where(inner_index == 0, key_rows, value_rows)
        piece = jnp.where(head_index == 0, kv[0], kv[1])
    with jax.named_scope("gather_kv"):
        gathered = lax.all_gather(piece, ("seq", "head", "inner"), axis=0, tiled=False)

    q_spec = pl.BlockSpec((2, rows, width), lambda h, sb: (0, 0, h))
    kv_spec = pl.BlockSpec((2, block_len, width), lambda h, sb: (0, 0, 0))
    acc_spec = pl.BlockSpec((2, 1, rows, 2 * width), lambda h, sb: (0, h, 0, 0))
    top_spec = pl.BlockSpec((2, 1, rows, width), lambda h, sb: (0, h, 0, 0))
    unit = 2 * rows * heads * block_len * width * 2
    acc, top = pl.pallas_call(
        functools.partial(local_kernel, coef),
        grid_spec=pltpu.PrefetchScalarGridSpec(
            num_scalar_prefetch=1,
            grid=(heads,),
            in_specs=[q_spec, kv_spec, kv_spec],
            out_specs=[acc_spec, top_spec],
        ),
        out_shape=[
            jax.ShapeDtypeStruct((2, heads, rows, 2 * width), jnp.float32),
            jax.ShapeDtypeStruct((2, heads, rows, width), jnp.float32),
        ],
        cost_estimate=pl.CostEstimate(flops=3 * unit, bytes_accessed=6_000_000, transcendentals=0),
        compiler_params=pltpu.CompilerParams(vmem_limit_bytes=48 * 1024 * 1024),
        name="local_part",
    )(slot_block, query_rows, key_rows, value_rows)

    attended, log_total = pl.pallas_call(
        functools.partial(remote_kernel, coef, count),
        grid_spec=pltpu.PrefetchScalarGridSpec(
            num_scalar_prefetch=1,
            grid=(heads,),
            in_specs=[q_spec, acc_spec, top_spec, pl.BlockSpec(memory_space=pl.ANY)],
            out_specs=[q_spec, pl.BlockSpec((2, heads, rows), lambda h, sb: (0, 0, 0))],
            scratch_shapes=[
                pltpu.VMEM((count, 2, block_len, width), jnp.bfloat16),
                pltpu.VMEM((count, 2, block_len, 2 * width), jnp.bfloat16),
                pltpu.VMEM((2, rows, 2 * width), jnp.float32),
                pltpu.VMEM((2, rows, width), jnp.float32),
                pltpu.SemaphoreType.DMA((count, 2, 2)),
            ],
        ),
        out_shape=[
            jax.ShapeDtypeStruct(query_rows.shape, query_rows.dtype),
            jax.ShapeDtypeStruct((2, heads, rows), jnp.float32),
        ],
        cost_estimate=pl.CostEstimate(flops=2 * (count - 1) * unit, bytes_accessed=8_000_000, transcendentals=0),
        compiler_params=pltpu.CompilerParams(vmem_limit_bytes=48 * 1024 * 1024),
        name="remote_part",
    )(slot_block, query_rows, acc, top, gathered)
    return attended, log_total


def solution(mesh):
    placed = (
        P(("groups", "seq"), "inner", "head"),
        P(("groups", "seq"), None, None),
        P(("groups", "seq"), None, None),
        P(),
    )
    return jax.shard_map(
        body,
        mesh=mesh,
        in_specs=placed,
        out_specs=(P(("groups", "seq"), "inner", "head"), P(("groups", "seq"), "head", "inner")),
        check_vma=False,
    )
```

time: 206 us -> 77.9 us (0.38); the launches traced: 208 us -> 77.5 us
  waiting for transfers between devices: 106 us -> 36.3 us
  matrix products: 28.5 us -> 0 us
  other arithmetic: 25.7 us -> 1.71 us
  starting transfers between devices: 21.2 us -> 0.04 us
  Pallas kernels: 0 us -> 19.3 us
  between operations: 2.01 us -> 14.1 us
  loops' own time: 11.4 us -> 0 us
  local copies, waits for them, and re-layouts: 13 us -> 6.06 us
    ppermute x16 -> x0, waiting for transfers between devices: 106 us -> none  [from_behind(): return lax.ppermute(block, axis, route)]
    all_gather x0 -> x1, waiting for transfers between devices: none -> 36.3 us  [body(): lax.all_gather(piece, ('seq', 'head', 'inner'), axis=0, tiled=False)]
    dot_general x16 -> x0, matrix products: 28.5 us -> none  [the longest x8 18.2 us: update(): jnp.einsum('hrc,cd->hrd', weights.astype(jnp.bfloat16), value_block, pref...]
    ppermute x16 -> x0, starting transfers between devices: 21.2 us -> none  [from_behind(): return lax.ppermute(block, axis, route)]
    pallas_call x0 -> x2, Pallas kernels: none -> 19.3 us  [the longest x1 12.6 us: body(): pl.pallas_call(functools.partial(remote_kernel, coef, count), grid_spec=p...]
    reduce_sum x8 -> x0, other arithmetic: 12.9 us -> none  [update(): total_new = total_run * shrink + jnp.sum(weights, axis=-1)]
    another operation x9 -> x0, loops' own time: 11.4 us -> none  [the longest x1 11 us: body(): lax.fori_loop(0, seq_count, cycle_step, (home_queries, empty))]
    squeeze x4 -> x0, local copies, waits for them, and re-layouts: 6.74 us -> none  [local_keys(): value_rows[slot]]
  transfers between devices with their start and end apart: 16 -> 1, of which waited for: 4 -> 1; matrix products, arithmetic and copies ran while one was open for 0% -> 0% of each run, Pallas kernels for 0% -> 9%
where the time goes in v1:
time: 77.9 us; the launch traced here: 77.5 us
  waiting for transfers between devices  36.3 us (47%)
  Pallas kernels  19.3 us (25%)
  between operations  14.1 us (18%)
  local copies, waits for them, and re-layouts  6.06 us (8%)
  other arithmetic  1.71 us (2%)
    all_gather x1, waiting for transfers between devices, body(): lax.all_gather(piece, ('seq', 'head', 'inner'), axis=0, tiled=False)  36.3 us
    pallas_call x1, Pallas kernels, body(): pl.pallas_call(functools.partial(remote_kernel, coef, count), grid_spec=p...  12.6 us
    pallas_call x1, Pallas kernels, body(): pl.pallas_call(functools.partial(local_kernel, coef), grid_spec=pltpu.Pre...  6.74 us
    unnamed x16, local copies, waits for them, and re-layouts  6.06 us
  transfers between devices with their start and end apart: 1, of which 1 were waited for; matrix products, arithmetic and copies ran while one was open for 0% of the time, Pallas kernels for 9%

profile of v1, /device:TPU:0, one launch (start us, length us, event | category | flops | bytes accessed | tf_op | source)
XLA Modules:
  0.0 77.5 jit_solution(2746175752478044805)
XLA Ops:
  7.2 0.0 all-gather.2.cloned.1.call-start
  7.2 1.0 %broadcast_select_fusion = bf16[2,640,128]{2,1,0:T(8,128)(2,1)S(1)} fusion(bf16[2,640,128]{2,1,0:T(8,128)(2,1)} %k_ref.1, bf16[2,640,128]{2,1,0:T(8,128)(2,1)} %v_ref.1, pred[]{:T(512)S(6)} %eq.7), kind=kLoop, calls=%fused_computation | loop fusion | flops 163840 | bytes 983041 | tf_op jit(solution)/shard_map/pieces/jit(_where)/select_n | solution.py:167
  8.2 0.0 copy-start.3
  8.3 0.0 copy-start.5
  8.3 0.7 slice_select_fusion
  9.0 0.0 all-gather.2.cloned.1.call-update
  9.0 0.0 copy-start
  9.0 1.0 %copy-done = bf16[2,640,128]{2,1,0:T(8,128)(2,1)S(1)} copy-done((bf16[2,640,128]{2,1,0:T(8,128)(2,1)S(1)}, bf16[2,640,128]{2,1,0:T(8,128)(2,1)}, u32[]{:S(2)}) %copy-start) | copy-done | bytes 327704
  10.0 0.0 copy-start.1
  10.0 1.0 %copy-done.1 = bf16[2,640,128]{2,1,0:T(8,128)(2,1)S(1)} copy-done((bf16[2,640,128]{2,1,0:T(8,128)(2,1)S(1)}, bf16[2,640,128]{2,1,0:T(8,128)(2,1)}, u32[]{:S(2)}) %copy-start.1) | copy-done | bytes 327704
  10.9 0.0 copy-start.2
  10.9 1.1 %copy-done.2 = bf16[2,320,512]{2,1,0:T(8,128)(2,1)S(1)} copy-done((bf16[2,320,512]{2,1,0:T(8,128)(2,1)S(1)}, bf16[2,320,512]{2,1,0:T(8,128)(2,1)}, u32[]{:S(2)}) %copy-start.2) | copy-done | bytes 655384
  12.0 0.0 copy-start.4
  12.0 0.7 copy-done.4
  12.7 6.7 %local_part.1 = (f32[2,4,320,256]{3,2,1,0:T(8,128)S(1)}, f32[2,4,320,128]{3,2,1,0:T(8,128)S(1)}) custom-call(s32[8]{0:T(128)S(1)} %copy-done.4, bf16[2,320,512]{2,1,0:T(8,128)(2,1)S(1)} %copy-done.2, bf16[2,640,128]{2,1,0:T(8,128)(2,1)S(1)} %copy-done, bf16[2,640,128]{2,1,0:T(8,128)(2,1)S(1)} %copy-done.1), custom_call_target="tpu_custom_call" | custom-call | flops 1258291200 | bytes 6000000 | tf_op jit(solution)/shard_map/local_part/pallas_call | solution.py:177
  19.4 0.0 copy-start.6
  19.4 1.0 %copy-done.6 = f32[2,4,320,128]{3,2,1,0:T(8,128)} copy-done((f32[2,4,320,128]{3,2,1,0:T(8,128)}, f32[2,4,320,128]{3,2,1,0:T(8,128)S(1)}, u32[]{:S(2)}) %copy-start.6) | copy-done | bytes 1310744
  20.5 36.3 %all-gather.2.cloned.1.call-done.kv_hbm = bf16[16,640,128]{2,1,0:T(8,128)(2,1)} async-done(((bf16[1,640,128]{2,1,0:T(8,128)(2,1)}), bf16[16,640,128]{2,1,0:T(8,128)(2,1)}) %all-gather.2.cloned.1.call-update) | async-done | bytes 2621456 | tf_op jit(solution)/shard_map/gather_kv/all_gather | solution.py:170
  56.8 0.0 copy-done.3
  56.8 0.0 copy-done.5
  56.8 0.0 copy-start.7
  56.8 1.3 %copy-done.7 = f32[2,4,320,128]{3,2,1,0:T(8,128)S(1)} copy-done((f32[2,4,320,128]{3,2,1,0:T(8,128)S(1)}, f32[2,4,320,128]{3,2,1,0:T(8,128)}, u32[]{:S(2)}) %copy-start.7) | copy-done | bytes 1310744
  58.1 12.6 %remote_part.1 = (bf16[2,320,512]{2,1,0:T(8,128)(2,1)}, f32[2,4,320]{2,1,0:T(4,128)}) custom-call(s32[8]{0:T(128)S(1)} %copy-done.5, bf16[2,320,512]{2,1,0:T(8,128)(2,1)S(1)} %copy-done.3, f32[2,4,320,256]{3,2,1,0:T(8,128)S(1)} %get-tuple-element.4.acc_in, f32[2,4,320,128]{3,2,1,0:T(8,128)S(1)} %copy-done.7, ...), custom_call_target="tpu_custom_call" | custom-call | flops 2516582400 | bytes 8000000 | tf_op jit(solution)/shard_map/remote_part/pallas_call | solution.py:194
Async XLA Ops:
  7.2 49.6 %all-gather.2.cloned.1.call-start = ((), (), s32[]{:S(2)}) async-start(), calls=%async_computation | async-start | bytes 2785280 | tf_op jit(solution)/shard_map/gather_kv/all_gather | solution.py:170
  8.2 48.5 %copy-start.3 = (bf16[2,320,512]{2,1,0:T(8,128)(2,1)S(1)}, bf16[2,320,512]{2,1,0:T(8,128)(2,1)}, u32[]{:S(2)}) copy-start(bf16[2,320,512]{2,1,0:T(8,128)(2,1)} %q_ref.3) | copy-start | bytes 1966084
  8.3 48.5 %copy-start.5 = (s32[8]{0:T(128)S(1)}, s32[8]{0:T(128)}, u32[]{:S(2)}) copy-start(s32[8]{0:T(128)} %sb.3) | copy-start | bytes 100
  9.0 1.0 %copy-start = (bf16[2,640,128]{2,1,0:T(8,128)(2,1)S(1)}, bf16[2,640,128]{2,1,0:T(8,128)(2,1)}, u32[]{:S(2)}) copy-start(bf16[2,640,128]{2,1,0:T(8,128)(2,1)} %k_ref.1) | copy-start | bytes 983044
  10.0 1.0 %copy-start.1 = (bf16[2,640,128]{2,1,0:T(8,128)(2,1)S(1)}, bf16[2,640,128]{2,1,0:T(8,128)(2,1)}, u32[]{:S(2)}) copy-start(bf16[2,640,128]{2,1,0:T(8,128)(2,1)} %v_ref.1) | copy-start | bytes 983044
  10.9 1.1 %copy-start.2 = (bf16[2,320,512]{2,1,0:T(8,128)(2,1)S(1)}, bf16[2,320,512]{2,1,0:T(8,128)(2,1)}, u32[]{:S(2)}) copy-start(bf16[2,320,512]{2,1,0:T(8,128)(2,1)} %q_ref.3) | copy-start | bytes 1966084
  12.0 0.7 copy-start.4
  19.4 1.1 %copy-start.6 = (f32[2,4,320,128]{3,2,1,0:T(8,128)}, f32[2,4,320,128]{3,2,1,0:T(8,128)S(1)}, u32[]{:S(2)}) copy-start(f32[2,4,320,128]{3,2,1,0:T(8,128)S(1)} %get-tuple-element.5.top_ref) | copy-start | bytes 3932164
  56.8 1.3 %copy-start.7 = (f32[2,4,320,128]{3,2,1,0:T(8,128)S(1)}, f32[2,4,320,128]{3,2,1,0:T(8,128)}, u32[]{:S(2)}) copy-start(f32[2,4,320,128]{3,2,1,0:T(8,128)} %copy-done.6) | copy-start | bytes 3932164
Sparse Core Ops, SparseCore 0:
  10.9 45.8 all-gather.1

commit v2 on v1

v2 whole, which is shorter than its diff:
```python
import functools
import math

import jax
import jax.numpy as jnp
from jax import lax
from jax.experimental import pallas as pl
from jax.experimental.pallas import tpu as pltpu
from jax.sharding import PartitionSpec as P

NEG = -1e30
SUM_LIMIT = 1e36


def score_dot(q, k):
    return lax.dot_general(q, k, (((1,), (1,)), ((), ())), preferred_element_type=jnp.float32)


def value_dot(p, v):
    return jnp.dot(p, v, preferred_element_type=jnp.float32)


def widen(x, width):
    return jnp.concatenate([x] * (width // x.shape[1]), axis=1)


def with_ones(x):
    return jnp.concatenate([x, jnp.ones_like(x)], axis=1)


def partner(index, distance, count):
    if count & (count - 1) == 0:
        return index ^ distance
    return (index + distance) % count


def source_of(index, distance, count):
    if count & (count - 1) == 0:
        return index ^ distance
    return lax.rem(index - distance + count, count)


def high_slot(sb, seq_index):
    b0, b1 = sb[2 * seq_index], sb[2 * seq_index + 1]
    return jnp.where(b1 > b0, 1, 0), jnp.maximum(b0, b1)


def minus_columns(top):
    high = top.astype(jnp.bfloat16)
    rest = top - high.astype(jnp.float32)
    middle = rest.astype(jnp.bfloat16)
    low = (rest - middle.astype(jnp.float32)).astype(jnp.bfloat16)
    lane = lax.broadcasted_iota(jnp.int32, top.shape, 1)
    high, middle, low = (x.astype(jnp.float32) for x in (high, middle, low))
    picked = jnp.where(lane == 0, high, jnp.where(lane == 1, middle, jnp.where(lane == 2, low, 0.0)))
    return (-picked).astype(jnp.bfloat16)


def local_kernel(coef, sb, q_ref, k_ref, v_ref, qx_ref, acc_ref):
    rows, block_len, width = q_ref.shape[1], k_ref.shape[1], k_ref.shape[2]
    inner = lax.axis_index("inner")
    hi, _ = high_slot(sb, lax.axis_index("seq"))
    lo = 1 - hi
    row = lax.broadcasted_iota(jnp.int32, (rows, block_len), 0) + inner * rows
    col = lax.broadcasted_iota(jnp.int32, (rows, block_len), 1)
    causal = col <= row

    def lanes_max(s):
        return jnp.broadcast_to(jnp.max(s, axis=1, keepdims=True), (rows, width))

    def weights(s, wide):
        return jnp.exp2((s - wide) * coef).astype(jnp.bfloat16)

    q_hi, q_lo = q_ref[hi], q_ref[lo]
    s_diag = jnp.where(causal, score_dot(q_hi, k_ref[hi]), NEG)
    s_past = score_dot(q_hi, k_ref[lo])
    s_low = jnp.where(causal, score_dot(q_lo, k_ref[lo]), NEG)
    top = lanes_max(jnp.maximum(s_diag, s_past))
    wide = widen(top, block_len)
    v_hi, v_lo = with_ones(v_ref[hi]), with_ones(v_ref[lo])
    acc = value_dot(weights(s_diag, wide), v_hi)
    top_low = lanes_max(s_low)
    acc += value_dot(weights(s_past, wide), v_lo)
    acc_low = value_dot(weights(s_low, widen(top_low, block_len)), v_lo)
    acc_ref[hi, 0] = acc
    acc_ref[lo, 0] = acc_low
    qx_ref[hi, 0] = jnp.concatenate([q_hi, minus_columns(top)], axis=1)
    qx_ref[lo, 0] = jnp.concatenate([q_lo, minus_columns(top_low)], axis=1)


def visit(coef, distance, sb, qx_ref, acc_in, parts, k_buf, v_buf, acc_out):
    width = qx_ref.shape[3] // 2
    count = lax.axis_size("seq")
    me = lax.axis_index("seq")
    head_index = lax.axis_index("head")
    inner = lax.axis_index("inner")
    hi, top_block = high_slot(sb, me)

    @pl.when(pl.program_id(0) == 0)
    def _():
        k_buf[:, :, width:] = jnp.ones((2, k_buf.shape[1], width), jnp.bfloat16)
        v_buf[:, :, width:] = jnp.ones((2, k_buf.shape[1], width), jnp.bfloat16)
        for value, (own_buf, twin_buf) in enumerate([(k_buf, v_buf), (v_buf, k_buf)]):

            @pl.when(inner == value)
            def _():
                for turn in range(2):
                    slot = head_index if turn == 0 else 1 - head_index
                    own_buf[slot, :, :width] = parts[turn][...]
                    twin_buf[slot, :, :width] = parts[2 + turn][...]

    other_hi, other_top = high_slot(sb, source_of(me, distance, count))
    above = top_block > other_top
    q_slot = jnp.where(above, hi, 1 - hi)
    k_slot = jnp.where(above, other_hi, 1 - other_hi)

    def weights(s):
        return jnp.exp2(s * coef).astype(jnp.bfloat16)

    acc_out[...] = acc_in[:, 0]
    s_first = score_dot(qx_ref[hi, 0], k_buf[1 - other_hi])
    s_second = score_dot(qx_ref[q_slot, 0], k_buf[k_slot])
    acc_out[hi] += value_dot(weights(s_first), v_buf[1 - other_hi])
    acc_out[q_slot] += value_dot(weights(s_second), v_buf[k_slot])


def middle_kernel(coef, distance, sb, qx_ref, acc_in, p0, p1, p2, p3, acc_out, k_buf, v_buf, acc):
    visit(coef, distance, sb, qx_ref, acc_in, (p0, p1, p2, p3), k_buf, v_buf, acc)
    acc_out[:, 0] = acc[...]


def last_kernel(coef, distance, distances, sb, qx_ref, acc_in, p0, p1, p2, p3, *rest):
    every = rest[: 4 * len(distances) + 2]
    out_ref, lse_ref, k_buf, v_buf, acc, run_top, sem = rest[4 * len(distances) + 2 :]
    visit(coef, distance, sb, qx_ref, acc_in, (p0, p1, p2, p3), k_buf, v_buf, acc)
    _, rows, width = run_top.shape
    block_len = k_buf.shape[1]
    count = lax.axis_size("seq")
    me = lax.axis_index("seq")
    head_index = lax.axis_index("head")
    inner = lax.axis_index("inner")
    fits = jnp.max(acc[:, :, width:]) < SUM_LIMIT

    @pl.when(fits)
    def _():
        for slot in range(2):
            minus = jnp.sum(qx_ref[slot, 0, :, width:].astype(jnp.float32), axis=1, keepdims=True)
            run_top[slot] = jnp.broadcast_to(-minus, (rows, width))

    @pl.when(jnp.logical_not(fits))
    def _():
        run_top[...] = jnp.full_like(run_top, NEG)
        acc[...] = jnp.zeros_like(acc)

        def fetch(src, buf, slot):
            copy = pltpu.make_async_copy(src, buf.at[slot, :, pl.ds(0, width)], sem)
            copy.start()
            copy.wait()

        def online(source):
            @pl.loop(0, 4)
            def _(i):
                slot, q_slot = i // 2, lax.rem(i, 2)
                shift = (sb[2 * me + q_slot] - sb[2 * source + slot]) * block_len + inner * rows

                @pl.when(shift + rows > 0)
                def _():
                    s = score_dot(qx_ref[q_slot, 0, :, :width], k_buf[slot, :, :width])
                    row = lax.broadcasted_iota(jnp.int32, s.shape, 0) + shift
                    allowed = lax.broadcasted_iota(jnp.int32, s.shape, 1) <= row
                    s = jnp.where(allowed, s, NEG)
                    before = run_top[q_slot]
                    top = jnp.maximum(before, jnp.broadcast_to(jnp.max(s, axis=1, keepdims=True), before.shape))
                    p = jnp.where(allowed, jnp.exp2((s - widen(top, block_len)) * coef), 0.0)
                    run_top[q_slot] = top
                    shrink = widen(jnp.exp2((before - top) * coef), 2 * width)
                    acc[q_slot] = acc[q_slot] * shrink + value_dot(p.astype(jnp.bfloat16), v_buf[slot])

        for slot in range(2):
            fetch(every[0].at[slot], k_buf, slot)
            fetch(every[1].at[slot], v_buf, slot)
        online(me)
        for place, other in enumerate(distances):
            pieces = every[2 + 4 * place : 6 + 4 * place]
            for value, (own_buf, twin_buf) in enumerate([(k_buf, v_buf), (v_buf, k_buf)]):

                @pl.when(inner == value)
                def _():
                    for turn in range(2):
                        slot = head_index if turn == 0 else 1 - head_index
                        fetch(pieces[turn], own_buf, slot)
                        fetch(pieces[2 + turn], twin_buf, slot)

            online(source_of(me, other, count))

    for slot in range(2):
        sums = acc[slot, :, width:]
        out_ref[slot] = (acc[slot, :, :width] / sums).astype(out_ref.dtype)
        log_total = run_top[slot] * (coef * math.log(2.0)) + jnp.log(sums)
        lse_ref[slot, pl.ds(pl.program_id(0), 1), :] = jnp.transpose(log_total)[:1]


def body(query_rows, key_rows, value_rows, slot_block):
    _, block_len, width = key_rows.shape
    _, rows, feats = query_rows.shape
    heads = feats // width
    count = lax.axis_size("seq")
    coef = math.log2(math.e) / math.sqrt(width)
    distances = list(range(1, count))

    head_index, inner_index = lax.axis_index("head"), lax.axis_index("inner")
    with jax.named_scope("pieces"):
        held = [
            jnp.where(inner_index == 0, key_rows[slot], value_rows[slot]) for slot in range(2)
        ]
        piece = jnp.where(head_index == 0, held[0], held[1])
    swap = [(0, 1), (1, 0)]
    with jax.named_scope("along_seq"):
        arrived = [
            lax.ppermute(piece, "seq", [(i, partner(i, d, count)) for i in range(count)])
            for d in distances
        ]
    q_spec = pl.BlockSpec((2, rows, width), lambda h, sb: (0, 0, h))
    kv_spec = pl.BlockSpec((2, block_len, width), lambda h, sb: (0, 0, 0))
    head_spec = pl.BlockSpec((2, 1, rows, 2 * width), lambda h, sb: (0, h, 0, 0))
    piece_spec = pl.BlockSpec((block_len, width), lambda h, sb: (0, 0))
    any_spec = pl.BlockSpec(memory_space=pl.ANY)
    acc_shape = jax.ShapeDtypeStruct((2, heads, rows, 2 * width), jnp.float32)
    params = pltpu.CompilerParams(vmem_limit_bytes=40 * 1024 * 1024)
    unit = rows * heads * block_len * width * 4
    exps = rows * heads * block_len

    def cost(units, size):
        return pl.CostEstimate(flops=2 * units * unit, bytes_accessed=size, transcendentals=units * exps)

    qx, acc = pl.pallas_call(
        functools.partial(local_kernel, coef),
        grid_spec=pltpu.PrefetchScalarGridSpec(
            num_scalar_prefetch=1,
            grid=(heads,),
            in_specs=[q_spec, kv_spec, kv_spec],
            out_specs=[head_spec, head_spec],
        ),
        out_shape=[jax.ShapeDtypeStruct(acc_shape.shape, jnp.bfloat16), acc_shape],
        cost_estimate=cost(3, 6_000_000),
        compiler_params=params,
        name="local_part",
    )(slot_block, query_rows, key_rows, value_rows)

    buffers = [
        pltpu.VMEM((2, block_len, 2 * width), jnp.bfloat16),
        pltpu.VMEM((2, block_len, 2 * width), jnp.bfloat16),
        pltpu.VMEM((2, rows, 2 * width), jnp.float32),
    ]
    visitors = []

    def attend(acc, distance, pieces):
        return pl.pallas_call(
            functools.partial(middle_kernel, coef, distance),
            grid_spec=pltpu.PrefetchScalarGridSpec(
                num_scalar_prefetch=1,
                grid=(heads,),
                in_specs=[head_spec, head_spec] + [piece_spec] * 4,
                out_specs=head_spec,
                scratch_shapes=buffers,
            ),
            out_shape=acc_shape,
            input_output_aliases={2: 0},
            cost_estimate=cost(2, 7_000_000),
            compiler_params=params,
            name=f"visitor_{distance}",
        )(slot_block, qx, acc, *pieces)

    for place, own in enumerate(arrived):
        if place >= 2:
            acc = attend(acc, distances[place - 2], visitors[place - 2])
        own, acc = lax.optimization_barrier((own, acc))
        with jax.named_scope("along_head"):
            across = lax.ppermute(own, "head", swap)
        with jax.named_scope("along_inner"):
            visitors.append((own, across, lax.ppermute(own, "inner", swap), lax.ppermute(across, "inner", swap)))
    if count > 2:
        acc = attend(acc, distances[-2], visitors[-2])

    flat = [part for pieces in visitors for part in pieces]
    attended, log_total = pl.pallas_call(
        functools.partial(last_kernel, coef, distances[-1], distances),
        grid_spec=pltpu.PrefetchScalarGridSpec(
            num_scalar_prefetch=1,
            grid=(heads,),
            in_specs=[head_spec, head_spec] + [piece_spec] * 4 + [any_spec] * (2 + len(flat)),
            out_specs=[q_spec, pl.BlockSpec((2, heads, rows), lambda h, sb: (0, 0, 0))],
            scratch_shapes=buffers + [pltpu.VMEM((2, rows, width), jnp.float32), pltpu.SemaphoreType.DMA],
        ),
        out_shape=[
            jax.ShapeDtypeStruct(query_rows.shape, query_rows.dtype),
            jax.ShapeDtypeStruct((2, heads, rows), jnp.float32),
        ],
        cost_estimate=cost(2, 7_000_000),
        compiler_params=params,
        name="last_visitor",
    )(slot_block, qx, acc, *visitors[-1], key_rows, value_rows, *flat)
    return attended, log_total


def solution(mesh):
    placed = (
        P(("groups", "seq"), "inner", "head"),
        P(("groups", "seq"), None, None),
        P(("groups", "seq"), None, None),
        P(),
    )
    return jax.shard_map(
        body,
        mesh=mesh,
        in_specs=placed,
        out_specs=(P(("groups", "seq"), "inner", "head"), P(("groups", "seq"), "head", "inner")),
        check_vma=False,
    )
```

time: 77.9 us -> 53.3 us (0.68)
  waiting for transfers between devices: 36.3 us -> 11.7 us
  between operations: 14.1 us -> 0.72 us
  starting transfers between devices: 0.04 us -> 12.3 us
  Pallas kernels: 19.3 us -> 23.3 us
  local copies, waits for them, and re-layouts: 6.06 us -> 3.69 us
    all_gather x1 -> x0, waiting for transfers between devices: 36.3 us -> none  [body(): lax.all_gather(piece, ('seq', 'head', 'inner'), axis=0, tiled=False)]
    ppermute x0 -> x12, starting transfers between devices: none -> 12.3 us  [the longest x3 8.16 us: body(): lax.ppermute(piece, 'seq', [(i, partner(i, d, count)) for i in range(coun...]
    ppermute x0 -> x12, waiting for transfers between devices: none -> 11.7 us  [the longest x3 6.64 us: body(): lax.ppermute(piece, 'seq', [(i, partner(i, d, count)) for i in range(coun...]
    pallas_call x1 -> x3, Pallas kernels: 12.6 us -> 16.4 us  [the longest x2 9.53 us: attend(): pl.pallas_call(functools.partial(middle_kernel, coef, distance), grid_spe...]
    unnamed x16 -> x8, local copies, waits for them, and re-layouts: 6.06 us -> 3.69 us
    select_n x2 -> x1, other arithmetic: 1.71 us -> 1.19 us  [body(): piece = jnp.where(head_index == 0, held[0], held[1])]
  transfers between devices with their start and end apart: 1 -> 12, of which waited for: 1 -> 3; matrix products, arithmetic and copies ran while one was open for 0% -> 0% of each run, Pallas kernels for 9% -> 31%
where the time goes in v2:
time: 53.3 us; the launch traced here: 52.9 us
  Pallas kernels  23.3 us (44%)
  starting transfers between devices  12.3 us (23%)
  waiting for transfers between devices  11.7 us (22%)
  local copies, waits for them, and re-layouts  3.69 us (7%)
  other arithmetic  1.19 us (2%)
  between operations  0.72 us (1%)
    pallas_call x2, Pallas kernels, attend(): pl.pallas_call(functools.partial(middle_kernel, coef, distance), grid_spe...  9.53 us
    ppermute x3, starting transfers between devices, body(): lax.ppermute(piece, 'seq', [(i, partner(i, d, count)) for i in range(coun...  8.16 us
    pallas_call x1, Pallas kernels, body(): pl.pallas_call(functools.partial(last_kernel, coef, distances[-1], distan...  6.91 us
    pallas_call x1, Pallas kernels, body(): pl.pallas_call(functools.partial(local_kernel, coef), grid_spec=pltpu.Pre...  6.86 us
    ppermute x3, waiting for transfers between devices, body(): lax.ppermute(piece, 'seq', [(i, partner(i, d, count)) for i in range(coun...  6.64 us
    ppermute x3, waiting for transfers between devices, body(): across = lax.ppermute(own, 'head', swap)  5.07 us
    unnamed x8, local copies, waits for them, and re-layouts  3.69 us
    ppermute x3, starting transfers between devices, body(): across = lax.ppermute(own, 'head', swap)  3.64 us
  transfers between devices with their start and end apart: 12, of which 3 were waited for; matrix products, arithmetic and copies ran while one was open for 0% of the time, Pallas kernels for 31%

profile of v2, /device:TPU:0, one launch (start us, length us, event | category | flops | bytes accessed | tf_op | source)
XLA Modules:
  0.0 52.9 jit_solution(14243052079521805382)
XLA Ops:
  0.6 1.2 %select_bitcast_fusion = bf16[640,128]{1,0:T(8,128)(2,1)S(1)} fusion(bf16[2,640,128]{2,1,0:T(8,128)(2,1)} %rest_1_.1, bf16[2,640,128]{2,1,0:T(8,128)(2,1)} %rest_0_.1, pred[]{:T(512)S(6)} %eq.8, pred[]{:T(512)S(6)} %eq.7), kind=kLoop, calls=%fused_computation | loop fusion | flops 245760 | bytes 819202 | tf_op jit(solution)/shard_map/pieces/jit(_where)/select_n | solution.py:216
  1.8 3.1 %collective-permute-start.2 = (bf16[640,128]{1,0:T(8,128)(2,1)S(1)}, bf16[640,128]{1,0:T(8,128)(2,1)S(1)}, u32[]{:S(2)}, u32[]{:S(2)}) collective-permute-start(bf16[640,128]{1,0:T(8,128)(2,1)S(1)} %select_bitcast_fusion), channel_id=1, source_target_pairs={{0,4},{4,0},{8,12},{12,8},{1,5},{5,1},{9,13},{13,9},{2,6},{6,2},{1... | collective-permute-start | bytes 491528 | tf_op jit(solution)/shard_map/along_seq/ppermute | solution.py:220
  4.9 1.0 %copy-done = bf16[2,640,128]{2,1,0:T(8,128)(2,1)S(1)} copy-done((bf16[2,640,128]{2,1,0:T(8,128)(2,1)S(1)}, bf16[2,640,128]{2,1,0:T(8,128)(2,1)}, u32[]{:S(2)}) %copy-start) | copy-done | bytes 327704
  5.9 1.0 %copy-done.1 = bf16[2,640,128]{2,1,0:T(8,128)(2,1)S(1)} copy-done((bf16[2,640,128]{2,1,0:T(8,128)(2,1)S(1)}, bf16[2,640,128]{2,1,0:T(8,128)(2,1)}, u32[]{:S(2)}) %copy-start.1) | copy-done | bytes 327704
  6.9 0.7 %copy-done.2 = s32[8]{0:T(128)S(1)} copy-done((s32[8]{0:T(128)S(1)}, s32[8]{0:T(128)}, u32[]{:S(2)}) %copy-start.2) | copy-done | bytes 56
  7.5 1.1 %copy-done.3 = bf16[2,320,512]{2,1,0:T(8,128)(2,1)S(1)} copy-done((bf16[2,320,512]{2,1,0:T(8,128)(2,1)S(1)}, bf16[2,320,512]{2,1,0:T(8,128)(2,1)}, u32[]{:S(2)}) %copy-start.3) | copy-done | bytes 655384
  8.6 6.9 %local_part.1 = (bf16[2,4,320,256]{3,2,1,0:T(8,128)(2,1)S(1)}, f32[2,4,320,256]{3,2,1,0:T(8,128)S(1)}) custom-call(s32[8]{0:T(128)S(1)} %copy-done.2, bf16[2,320,512]{2,1,0:T(8,128)(2,1)S(1)} %copy-done.3, bf16[2,640,128]{2,1,0:T(8,128)(2,1)S(1)} %copy-done, bf16[2,640,128]{2,1,0:T(8,128)(2,1)S(1)} %copy-done.1), custom_call_target="tpu_custom_call" | custom-call | flops 2516582400 | bytes 6000000 | tf_op jit(solution)/shard_map/local_part/pallas_call | solution.py:236
  15.5 0.0 collective-permute-done.2.p0.rest_2_
  15.5 1.5 %collective-permute-start.3 = (bf16[640,128]{1,0:T(8,128)(2,1)S(1)}, bf16[640,128]{1,0:T(8,128)(2,1)S(1)}, u32[]{:S(2)}, u32[]{:S(2)}) collective-permute-start(bf16[640,128]{1,0:T(8,128)(2,1)S(1)} %collective-permute-done.2.p0.rest_2_), channel_id=1, source_target_pairs={{0,2},{2,0},{1,3},{3,1},{4,6},{6,4},{5,7},{7,5},{8,10},{10,8},{9,1... | collective-permute-start | bytes 491528 | tf_op jit(solution)/shard_map/along_head/ppermute | solution.py:279
  17.0 2.6 %collective-permute-start.1 = (bf16[640,128]{1,0:T(8,128)(2,1)S(1)}, bf16[640,128]{1,0:T(8,128)(2,1)S(1)}, u32[]{:S(2)}, u32[]{:S(2)}) collective-permute-start(bf16[640,128]{1,0:T(8,128)(2,1)S(1)} %select_bitcast_fusion), channel_id=1, source_target_pairs={{0,8},{4,12},{8,0},{12,4},{1,9},{5,13},{9,1},{13,5},{2,10},{6,14},... | collective-permute-start | bytes 491528 | tf_op jit(solution)/shard_map/along_seq/ppermute | solution.py:220
  19.6 0.0 collective-permute-start.4
  19.6 1.6 %collective-permute-done.3.p1.rest_3_ = bf16[640,128]{1,0:T(8,128)(2,1)S(1)} collective-permute-done((bf16[640,128]{1,0:T(8,128)(2,1)S(1)}, bf16[640,128]{1,0:T(8,128)(2,1)S(1)}, u32[]{:S(2)}, u32[]{:S(2)}) %collective-permute-start.3) | collective-permute-done | bytes 163872 | tf_op jit(solution)/shard_map/along_head/ppermute | solution.py:279
  21.2 0.0 collective-permute-start.5
  21.2 2.5 %collective-permute-start = (bf16[640,128]{1,0:T(8,128)(2,1)S(1)}, bf16[640,128]{1,0:T(8,128)(2,1)S(1)}, u32[]{:S(2)}, u32[]{:S(2)}) collective-permute-start(bf16[640,128]{1,0:T(8,128)(2,1)S(1)} %select_bitcast_fusion), channel_id=1, source_target_pairs={{0,12},{4,8},{8,4},{12,0},{1,13},{5,9},{9,5},{13,1},{2,14},{6,10},... | collective-permute-start | bytes 491528 | tf_op jit(solution)/shard_map/along_seq/ppermute | solution.py:220
  23.7 6.6 %collective-permute-done.1.p0.rest_6_ = bf16[640,128]{1,0:T(8,128)(2,1)S(1)} collective-permute-done((bf16[640,128]{1,0:T(8,128)(2,1)S(1)}, bf16[640,128]{1,0:T(8,128)(2,1)S(1)}, u32[]{:S(2)}, u32[]{:S(2)}) %collective-permute-start.1) | collective-permute-done | bytes 163872 | tf_op jit(solution)/shard_map/along_seq/ppermute | solution.py:220
  30.3 0.0 collective-permute-start.6
  30.3 0.0 collective-permute-done.4.p2.rest_4_
  30.3 0.0 collective-permute-done.5.p3.rest_5_
  30.3 4.8 %visitor_1.1.acc_in = f32[2,4,320,256]{3,2,1,0:T(8,128)S(1)} custom-call(s32[8]{0:T(128)S(1)} %copy-done.2, bf16[2,4,320,256]{3,2,1,0:T(8,128)(2,1)S(1)} %get-tuple-element.10.qx_ref, f32[2,4,320,256]{3,2,1,0:T(8,128)S(1)} %get-tuple-element.13.acc_in, bf16[640,128]{1,0:T(8,128)(2,1)S(1)} %collective-permute-done.2.p0.rest_2_, ...), custom_call_target="tpu_custom_call", output_to_operand_aliasing={{}: (2, {})} | custom-call | flops 1677721600 | bytes 7000000 | tf_op jit(solution)/shard_map/visitor_1/pallas_call | solution.py:258
  35.1 0.0 collective-permute-done.p0.rest_10_
  35.1 2.1 %collective-permute-start.9 = (bf16[640,128]{1,0:T(8,128)(2,1)S(1)}, bf16[640,128]{1,0:T(8,128)(2,1)S(1)}, u32[]{:S(2)}, u32[]{:S(2)}) collective-permute-start(bf16[640,128]{1,0:T(8,128)(2,1)S(1)} %collective-permute-done.p0.rest_10_), channel_id=1, source_target_pairs={{0,2},{2,0},{1,3},{3,1},{4,6},{6,4},{5,7},{7,5},{8,10},{10,8},{9,1... | collective-permute-start | bytes 491528 | tf_op jit(solution)/shard_map/along_head/ppermute | solution.py:279
  37.2 0.0 collective-permute-start.7
  37.2 0.0 collective-permute-done.6.p1.rest_7_
  37.2 0.5 collective-permute-start.8
  37.7 0.0 collective-permute-start.10
  37.7 3.5 %collective-permute-done.9.p1.rest_11_ = bf16[640,128]{1,0:T(8,128)(2,1)S(1)} collective-permute-done((bf16[640,128]{1,0:T(8,128)(2,1)S(1)}, bf16[640,128]{1,0:T(8,128)(2,1)S(1)}, u32[]{:S(2)}, u32[]{:S(2)}) %collective-permute-start.9) | collective-permute-done | bytes 163872 | tf_op jit(solution)/shard_map/along_head/ppermute | solution.py:279
  41.2 0.0 collective-permute-start.11
  41.2 0.0 collective-permute-done.7.p2.rest_8_
  41.2 0.0 collective-permute-done.8.p3.rest_9_
  41.2 4.8 %visitor_2.1.acc_in = f32[2,4,320,256]{3,2,1,0:T(8,128)S(1)} custom-call(s32[8]{0:T(128)S(1)} %copy-done.2, bf16[2,4,320,256]{3,2,1,0:T(8,128)(2,1)S(1)} %get-tuple-element.10.qx_ref, f32[2,4,320,256]{3,2,1,0:T(8,128)S(1)} %visitor_1.1.acc_in, bf16[640,128]{1,0:T(8,128)(2,1)S(1)} %collective-permute-done.1.p0.rest_6_, ...), custom_call_target="tpu_custom_call", output_to_operand_aliasing={{}: (2, {})} | custom-call | flops 1677721600 | bytes 7000000 | tf_op jit(solution)/shard_map/visitor_2/pallas_call | solution.py:258
  46.0 0.0 collective-permute-done.10.p2.rest_12_
  46.0 6.9 %last_visitor.1 = (bf16[2,320,512]{2,1,0:T(8,128)(2,1)}, f32[2,4,320]{2,1,0:T(4,128)}) custom-call(s32[8]{0:T(128)S(1)} %copy-done.2, bf16[2,4,320,256]{3,2,1,0:T(8,128)(2,1)S(1)} %get-tuple-element.10.qx_ref, f32[2,4,320,256]{3,2,1,0:T(8,128)S(1)} %visitor_2.1.acc_in, bf16[640,128]{1,0:T(8,128)(2,1)S(1)} %collective-permute-done.p0.rest_10_, ...), custom_call_target="tpu_custom_call" | custom-call | flops 1677721600 | bytes 7000000 | tf_op jit(solution)/shard_map/last_visitor/pallas_call | solution.py:286
  (5 shorter events, 0.0 us)
Async XLA Ops:
  1.8 13.6 %collective-permute-start.2 = (bf16[640,128]{1,0:T(8,128)(2,1)S(1)}, bf16[640,128]{1,0:T(8,128)(2,1)S(1)}, u32[]{:S(2)}, u32[]{:S(2)}) collective-permute-start(bf16[640,128]{1,0:T(8,128)(2,1)S(1)} %select_bitcast_fusion), channel_id=1, source_target_pairs={{0,4},{4,0},{8,12},{12,8},{1,5},{5,1},{9,13},{13,9},{2,6},{6,2},{1... | collective-permute-start | bytes 491528 | tf_op jit(solution)/shard_map/along_seq/ppermute | solution.py:220
  4.9 1.0 %copy-start = (bf16[2,640,128]{2,1,0:T(8,128)(2,1)S(1)}, bf16[2,640,128]{2,1,0:T(8,128)(2,1)}, u32[]{:S(2)}) copy-start(bf16[2,640,128]{2,1,0:T(8,128)(2,1)} %rest_0_.1) | copy-start | bytes 983044
  5.9 1.0 %copy-start.1 = (bf16[2,640,128]{2,1,0:T(8,128)(2,1)S(1)}, bf16[2,640,128]{2,1,0:T(8,128)(2,1)}, u32[]{:S(2)}) copy-start(bf16[2,640,128]{2,1,0:T(8,128)(2,1)} %rest_1_.1) | copy-start | bytes 983044
  6.9 0.7 %copy-start.2 = (s32[8]{0:T(128)S(1)}, s32[8]{0:T(128)}, u32[]{:S(2)}) copy-start(s32[8]{0:T(128)} %sb.7) | copy-start | bytes 100
  7.5 1.1 %copy-start.3 = (bf16[2,320,512]{2,1,0:T(8,128)(2,1)S(1)}, bf16[2,320,512]{2,1,0:T(8,128)(2,1)}, u32[]{:S(2)}) copy-start(bf16[2,320,512]{2,1,0:T(8,128)(2,1)} %q_ref.1) | copy-start | bytes 1966084
  15.5 5.7 %collective-permute-start.3 = (bf16[640,128]{1,0:T(8,128)(2,1)S(1)}, bf16[640,128]{1,0:T(8,128)(2,1)S(1)}, u32[]{:S(2)}, u32[]{:S(2)}) collective-permute-start(bf16[640,128]{1,0:T(8,128)(2,1)S(1)} %collective-permute-done.2.p0.rest_2_), channel_id=1, source_target_pairs={{0,2},{2,0},{1,3},{3,1},{4,6},{6,4},{5,7},{7,5},{8,10},{10,8},{9,1... | collective-permute-start | bytes 491528 | tf_op jit(solution)/shard_map/along_head/ppermute | solution.py:279
  17.0 13.3 %collective-permute-start.1 = (bf16[640,128]{1,0:T(8,128)(2,1)S(1)}, bf16[640,128]{1,0:T(8,128)(2,1)S(1)}, u32[]{:S(2)}, u32[]{:S(2)}) collective-permute-start(bf16[640,128]{1,0:T(8,128)(2,1)S(1)} %select_bitcast_fusion), channel_id=1, source_target_pairs={{0,8},{4,12},{8,0},{12,4},{1,9},{5,13},{9,1},{13,5},{2,10},{6,14},... | collective-permute-start | bytes 491528 | tf_op jit(solution)/shard_map/along_seq/ppermute | solution.py:220
  19.6 10.7 %collective-permute-start.4 = (bf16[640,128]{1,0:T(8,128)(2,1)S(1)}, bf16[640,128]{1,0:T(8,128)(2,1)S(1)}, u32[]{:S(2)}, u32[]{:S(2)}) collective-permute-start(bf16[640,128]{1,0:T(8,128)(2,1)S(1)} %collective-permute-done.2.p0.rest_2_), channel_id=1, source_target_pairs={{0,1},{1,0},{2,3},{3,2},{4,5},{5,4},{6,7},{7,6},{8,9},{9,8},{10,11... | collective-permute-start | bytes 491528 | tf_op jit(solution)/shard_map/along_inner/ppermute | solution.py:281
  21.2 9.1 %collective-permute-start.5 = (bf16[640,128]{1,0:T(8,128)(2,1)S(1)}, bf16[640,128]{1,0:T(8,128)(2,1)S(1)}, u32[]{:S(2)}, u32[]{:S(2)}) collective-permute-start(bf16[640,128]{1,0:T(8,128)(2,1)S(1)} %collective-permute-done.3.p1.rest_3_), channel_id=1, source_target_pairs={{0,1},{1,0},{2,3},{3,2},{4,5},{5,4},{6,7},{7,6},{8,9},{9,8},{10,11... | collective-permute-start | bytes 491528 | tf_op jit(solution)/shard_map/along_inner/ppermute | solution.py:281
  21.2 13.9 %collective-permute-start = (bf16[640,128]{1,0:T(8,128)(2,1)S(1)}, bf16[640,128]{1,0:T(8,128)(2,1)S(1)}, u32[]{:S(2)}, u32[]{:S(2)}) collective-permute-start(bf16[640,128]{1,0:T(8,128)(2,1)S(1)} %select_bitcast_fusion), channel_id=1, source_target_pairs={{0,12},{4,8},{8,4},{12,0},{1,13},{5,9},{9,5},{13,1},{2,14},{6,10},... | collective-permute-start | bytes 491528 | tf_op jit(solution)/shard_map/along_seq/ppermute | solution.py:220
  30.3 6.9 %collective-permute-start.6 = (bf16[640,128]{1,0:T(8,128)(2,1)S(1)}, bf16[640,128]{1,0:T(8,128)(2,1)S(1)}, u32[]{:S(2)}, u32[]{:S(2)}) collective-permute-start(bf16[640,128]{1,0:T(8,128)(2,1)S(1)} %collective-permute-done.1.p0.rest_6_), channel_id=1, source_target_pairs={{0,2},{2,0},{1,3},{3,1},{4,6},{6,4},{5,7},{7,5},{8,10},{10,8},{9,1... | collective-permute-start | bytes 491528 | tf_op jit(solution)/shard_map/along_head/ppermute | solution.py:279
  35.1 6.1 %collective-permute-start.9 = (bf16[640,128]{1,0:T(8,128)(2,1)S(1)}, bf16[640,128]{1,0:T(8,128)(2,1)S(1)}, u32[]{:S(2)}, u32[]{:S(2)}) collective-permute-start(bf16[640,128]{1,0:T(8,128)(2,1)S(1)} %collective-permute-done.p0.rest_10_), channel_id=1, source_target_pairs={{0,2},{2,0},{1,3},{3,1},{4,6},{6,4},{5,7},{7,5},{8,10},{10,8},{9,1... | collective-permute-start | bytes 491528 | tf_op jit(solution)/shard_map/along_head/ppermute | solution.py:279
  37.2 4.0 %collective-permute-start.7 = (bf16[640,128]{1,0:T(8,128)(2,1)S(1)}, bf16[640,128]{1,0:T(8,128)(2,1)S(1)}, u32[]{:S(2)}, u32[]{:S(2)}) collective-permute-start(bf16[640,128]{1,0:T(8,128)(2,1)S(1)} %collective-permute-done.1.p0.rest_6_), channel_id=1, source_target_pairs={{0,1},{1,0},{2,3},{3,2},{4,5},{5,4},{6,7},{7,6},{8,9},{9,8},{10,11... | collective-permute-start | bytes 491528 | tf_op jit(solution)/shard_map/along_inner/ppermute | solution.py:281
  37.2 4.0 %collective-permute-start.8 = (bf16[640,128]{1,0:T(8,128)(2,1)S(1)}, bf16[640,128]{1,0:T(8,128)(2,1)S(1)}, u32[]{:S(2)}, u32[]{:S(2)}) collective-permute-start(bf16[640,128]{1,0:T(8,128)(2,1)S(1)} %collective-permute-done.6.p1.rest_7_), channel_id=1, source_target_pairs={{0,1},{1,0},{2,3},{3,2},{4,5},{5,4},{6,7},{7,6},{8,9},{9,8},{10,11... | collective-permute-start | bytes 491528 | tf_op jit(solution)/shard_map/along_inner/ppermute | solution.py:281
  37.7 8.3 %collective-permute-start.10 = (bf16[640,128]{1,0:T(8,128)(2,1)S(1)}, bf16[640,128]{1,0:T(8,128)(2,1)S(1)}, u32[]{:S(2)}, u32[]{:S(2)}) collective-permute-start(bf16[640,128]{1,0:T(8,128)(2,1)S(1)} %collective-permute-done.p0.rest_10_), channel_id=1, source_target_pairs={{0,1},{1,0},{2,3},{3,2},{4,5},{5,4},{6,7},{7,6},{8,9},{9,8},{10,11... | collective-permute-start | bytes 491528 | tf_op jit(solution)/shard_map/along_inner/ppermute | solution.py:281
  41.2 4.8 %collective-permute-start.11 = (bf16[640,128]{1,0:T(8,128)(2,1)S(1)}, bf16[640,128]{1,0:T(8,128)(2,1)S(1)}, u32[]{:S(2)}, u32[]{:S(2)}) collective-permute-start(bf16[640,128]{1,0:T(8,128)(2,1)S(1)} %collective-permute-done.9.p1.rest_11_), channel_id=1, source_target_pairs={{0,1},{1,0},{2,3},{3,2},{4,5},{5,4},{6,7},{7,6},{8,9},{9,8},{10,11... | collective-permute-start | bytes 491528 | tf_op jit(solution)/shard_map/along_inner/ppermute | solution.py:281

commit v3 on v2

v3 whole, which is shorter than its diff:
```python
import functools
import math

import jax
import jax.numpy as jnp
from jax import lax
from jax.experimental import pallas as pl
from jax.experimental.pallas import tpu as pltpu
from jax.sharding import PartitionSpec as P

NEG = -1e30
SUM_LIMIT = 1e36
LO, HI = 0, 1


def score_dot(q, k):
    return lax.dot_general(q, k, (((1,), (1,)), ((), ())), preferred_element_type=jnp.float32)


def value_dot(p, v):
    return jnp.dot(p, v, preferred_element_type=jnp.float32)


def widen(x, width):
    return jnp.concatenate([x] * (width // x.shape[1]), axis=1)


def with_ones(x):
    return jnp.concatenate([x, jnp.ones_like(x)], axis=1)


def is_power(count):
    return count & (count - 1) == 0


def source_of(index, distance, count):
    if is_power(count):
        return index ^ distance
    return lax.rem(index - distance + count, count)


def blocks_of(sb, seq_index):
    b0, b1 = sb[2 * seq_index], sb[2 * seq_index + 1]
    return jnp.where(b1 > b0, 1, 0), jnp.minimum(b0, b1), jnp.maximum(b0, b1)


def minus_columns(top):
    high = top.astype(jnp.bfloat16)
    rest = top - high.astype(jnp.float32)
    middle = rest.astype(jnp.bfloat16)
    low = (rest - middle.astype(jnp.float32)).astype(jnp.bfloat16)
    lane = lax.broadcasted_iota(jnp.int32, top.shape, 1)
    high, middle, low = (x.astype(jnp.float32) for x in (high, middle, low))
    picked = jnp.where(lane == 0, high, jnp.where(lane == 1, middle, jnp.where(lane == 2, low, 0.0)))
    return (-picked).astype(jnp.bfloat16)


def local_kernel(coef, sb, q_hbm, k_hbm, v_hbm, qx_ref, acc_ref, q_buf, k_buf, v_buf, sems):
    heads = qx_ref.shape[1]
    _, block_len, width = k_buf.shape
    rows = q_buf.shape[1]
    inner = lax.axis_index("inner")
    hi, _, _ = blocks_of(sb, lax.axis_index("seq"))
    copies = []
    for place, (src, dst) in enumerate([(k_hbm, k_buf), (q_hbm, q_buf), (v_hbm, v_buf)]):
        for order, slot in ((LO, 1 - hi), (HI, hi)):
            copies.append(pltpu.make_async_copy(src.at[slot], dst.at[order], sems.at[place, order]))
    for copy in copies:
        copy.start()
    row = lax.broadcasted_iota(jnp.int32, (rows, block_len), 0) + inner * rows
    col = lax.broadcasted_iota(jnp.int32, (rows, block_len), 1)
    causal = col <= row

    def lanes_max(s):
        return jnp.broadcast_to(jnp.max(s, axis=1, keepdims=True), (rows, width))

    def weights(s, top):
        return jnp.exp2((s - widen(top, block_len)) * coef).astype(jnp.bfloat16)

    for copy in copies[:4]:
        copy.wait()

    def scores(h):
        q_lo = q_buf[LO, :, h * width : (h + 1) * width]
        q_hi = q_buf[HI, :, h * width : (h + 1) * width]
        past = score_dot(q_hi, k_buf[LO])
        diag = jnp.where(causal, score_dot(q_hi, k_buf[HI]), NEG)
        low = jnp.where(causal, score_dot(q_lo, k_buf[LO]), NEG)
        return q_lo, q_hi, past, diag, low

    ready = scores(0)
    for copy in copies[4:]:
        copy.wait()
    for h in range(heads):
        q_lo, q_hi, past, diag, low = ready
        if h + 1 < heads:
            ready = scores(h + 1)
        v_lo, v_hi = with_ones(v_buf[LO]), with_ones(v_buf[HI])
        top = lanes_max(jnp.maximum(past, diag))
        acc_ref[HI, h] = value_dot(weights(past, top), v_lo) + value_dot(weights(diag, top), v_hi)
        qx_ref[HI, h] = jnp.concatenate([q_hi, minus_columns(top)], axis=1)
        top = lanes_max(low)
        acc_ref[LO, h] = value_dot(weights(low, top), v_lo)
        qx_ref[LO, h] = jnp.concatenate([q_lo, minus_columns(top)], axis=1)


def visit(coef, distance, sb, qx_ref, acc_ref, parts, k_buf, v_buf):
    _, heads, rows, _ = qx_ref.shape
    _, block_len, width = k_buf.shape
    count = lax.axis_size("seq")
    me = lax.axis_index("seq")
    head_index = lax.axis_index("head")
    inner = lax.axis_index("inner")
    for value, (own_buf, twin_buf) in enumerate([(k_buf, v_buf), (v_buf, k_buf)]):

        @pl.when(inner == value)
        def _():
            for turn in range(2):
                slot = head_index if turn == 0 else 1 - head_index
                own_buf[slot] = parts[turn][...]
                twin_buf[slot] = parts[2 + turn][...]

    _, _, top_block = blocks_of(sb, me)
    other_hi, _, other_top = blocks_of(sb, source_of(me, distance, count))
    other_lo = 1 - other_hi
    above = top_block > other_top

    def weights(s):
        return jnp.exp2(s * coef).astype(jnp.bfloat16)

    def in_turn(chunks, score, finish):
        ready = score(*chunks[0])
        for place, chunk in enumerate(chunks):
            now = ready
            if place + 1 < len(chunks):
                ready = score(*chunks[place + 1])
            finish(weights(now), *chunk)

    @pl.when(above)
    def _():
        def score(h):
            return score_dot(qx_ref[HI, h], with_ones(k_buf[...].reshape(2 * block_len, width)))

        def finish(p, h):
            acc_ref[HI, h] += value_dot(p, with_ones(v_buf[...].reshape(2 * block_len, width)))

        in_turn([(h,) for h in range(heads)], score, finish)

    @pl.when(jnp.logical_not(above))
    def _():
        def score(h, order):
            return score_dot(qx_ref[order, h], with_ones(k_buf[other_lo]))

        def finish(p, h, order):
            acc_ref[order, h] += value_dot(p, with_ones(v_buf[other_lo]))

        in_turn([(h, order) for h in range(heads) for order in (HI, LO)], score, finish)


def middle_kernel(coef, distance, sb, qx_ref, acc_in, p0, p1, p2, p3, acc_ref, k_buf, v_buf):
    visit(coef, distance, sb, qx_ref, acc_ref, (p0, p1, p2, p3), k_buf, v_buf)


def last_kernel(coef, distance, distances, sb, qx_ref, acc_ref, p0, p1, p2, p3, *rest):
    every = rest[: 4 * len(distances) + 2]
    out_ref, lse_ref, k_buf, v_buf, run_top, run_acc, sem = rest[4 * len(distances) + 2 :]
    visit(coef, distance, sb, qx_ref, acc_ref, (p0, p1, p2, p3), k_buf, v_buf)
    _, heads, rows, _ = qx_ref.shape
    _, block_len, width = k_buf.shape
    count = lax.axis_size("seq")
    me = lax.axis_index("seq")
    head_index = lax.axis_index("head")
    inner = lax.axis_index("inner")
    hi, lo_block, hi_block = blocks_of(sb, me)

    def first_row(x):
        return jnp.transpose(x)[:1]

    def emit(order, h, acc, top_row):
        slot = hi if order == HI else 1 - hi
        sums = acc[:, width:]
        out_ref[slot, :, h * width : (h + 1) * width] = (acc[:, :width] / sums).astype(out_ref.dtype)
        lse_ref[slot, h : h + 1, :] = top_row * (coef * math.log(2.0)) + jnp.log(first_row(sums))

    for order in (LO, HI):
        for h in range(heads):
            columns = jnp.transpose(qx_ref[order, h, :, width:].astype(jnp.float32))
            emit(order, h, acc_ref[order, h], -(columns[0:1] + columns[1:2] + columns[2:3]))

    @pl.when(jnp.logical_not(jnp.max(acc_ref[:, :, :, width:]) < SUM_LIMIT))
    def _():
        def fetch(src, buf, slot):
            copy = pltpu.make_async_copy(src, buf.at[slot], sem)
            copy.start()
            copy.wait()

        def online(source):
            @pl.loop(0, 4 * heads)
            def _(i):
                h, slot, order = i // 4, lax.rem(i, 4) // 2, lax.rem(i, 2)
                own_block = jnp.where(order == HI, hi_block, lo_block)
                shift = (own_block - sb[2 * source + slot]) * block_len + inner * rows

                @pl.when(shift + rows > 0)
                def _():
                    s = score_dot(qx_ref[order, h, :, :width], k_buf[slot])
                    row = lax.broadcasted_iota(jnp.int32, s.shape, 0) + shift
                    allowed = lax.broadcasted_iota(jnp.int32, s.shape, 1) <= row
                    s = jnp.where(allowed, s, NEG)
                    before = run_top[order, h]
                    top = jnp.maximum(before, jnp.broadcast_to(jnp.max(s, axis=1, keepdims=True), before.shape))
                    p = jnp.where(allowed, jnp.exp2((s - widen(top, block_len)) * coef), 0.0)
                    run_top[order, h] = top
                    shrink = widen(jnp.exp2((before - top) * coef), 2 * width)
                    part = value_dot(p.astype(jnp.bfloat16), with_ones(v_buf[slot]))
                    run_acc[order, h] = run_acc[order, h] * shrink + part

        run_top[...] = jnp.full_like(run_top, NEG)
        run_acc[...] = jnp.zeros_like(run_acc)
        for slot in range(2):
            fetch(every[0].at[slot], k_buf, slot)
            fetch(every[1].at[slot], v_buf, slot)
        online(me)
        for place, other in enumerate(distances):
            pieces = every[2 + 4 * place : 6 + 4 * place]
            for value, (own_buf, twin_buf) in enumerate([(k_buf, v_buf), (v_buf, k_buf)]):

                @pl.when(inner == value)
                def _():
                    for turn in range(2):
                        slot = head_index if turn == 0 else 1 - head_index
                        fetch(pieces[turn], own_buf, slot)
                        fetch(pieces[2 + turn], twin_buf, slot)

            online(source_of(me, other, count))
        for order in (LO, HI):
            for h in range(heads):
                emit(order, h, run_acc[order, h], first_row(run_top[order, h]))


def body(query_rows, key_rows, value_rows, slot_block):
    _, block_len, width = key_rows.shape
    _, rows, feats = query_rows.shape
    heads = feats // width
    count = lax.axis_size("seq")
    coef = math.log2(math.e) / math.sqrt(width)
    distances = list(range(1, count))
    swap = [(0, 1), (1, 0)]

    def along_seq(block, distance):
        if is_power(count):
            route = [(i, i ^ distance) for i in range(count)]
        else:
            route = [(i, (i + distance) % count) for i in range(count)]
        with jax.named_scope("along_seq"):
            return lax.ppermute(block, "seq", route)

    head_index, inner_index = lax.axis_index("head"), lax.axis_index("inner")
    with jax.named_scope("pieces"):
        held = [
            jnp.where(inner_index == 0, key_rows[slot], value_rows[slot]) for slot in range(2)
        ]
        piece = jnp.where(head_index == 0, held[0], held[1])
    arrived = {}
    for distance in distances:
        if not is_power(count) or is_power(distance):
            arrived[distance] = along_seq(piece, distance)

    whole = pl.BlockSpec(memory_space=pltpu.VMEM)
    anywhere = pl.BlockSpec(memory_space=pl.ANY)
    in_hbm = pl.BlockSpec(memory_space=pltpu.HBM)
    scalars = pl.BlockSpec(memory_space=pltpu.SMEM)
    acc_shape = jax.ShapeDtypeStruct((2, heads, rows, 2 * width), jnp.float32)
    qx_shape = jax.ShapeDtypeStruct(acc_shape.shape, jnp.bfloat16)
    params = pltpu.CompilerParams(vmem_limit_bytes=40 * 1024 * 1024)
    unit = rows * heads * block_len * width * 4
    exps = rows * heads * block_len

    def cost(units, size):
        return pl.CostEstimate(flops=2 * units * unit, bytes_accessed=size, transcendentals=units * exps)

    kv_buffers = [pltpu.VMEM((2, block_len, width), jnp.bfloat16)] * 2
    qx, acc = pl.pallas_call(
        functools.partial(local_kernel, coef),
        in_specs=[scalars] + [in_hbm] * 3,
        out_specs=[whole, whole],
        out_shape=[qx_shape, acc_shape],
        scratch_shapes=[pltpu.VMEM((2, rows, feats), jnp.bfloat16)] + kv_buffers + [pltpu.SemaphoreType.DMA((3, 2))],
        cost_estimate=cost(3, 6_000_000),
        compiler_params=params,
        name="local_part",
    )(slot_block, query_rows, key_rows, value_rows)

    def attend(acc, distance):
        return pl.pallas_call(
            functools.partial(middle_kernel, coef, distance),
            in_specs=[scalars] + [whole] * 6,
            out_specs=whole,
            out_shape=acc_shape,
            scratch_shapes=kv_buffers,
            input_output_aliases={2: 0},
            cost_estimate=cost(2, 7_000_000),
            compiler_params=params,
            name=f"visitor_{distance}",
        )(slot_block, qx, acc, *visitors[distance])

    visitors = {}
    first, acc = lax.optimization_barrier((arrived, acc))
    arrived = dict(first)
    for place, distance in enumerate(distances):
        if distance not in arrived:
            near = distance & -distance
            arrived[distance] = along_seq(arrived[distance ^ near], near)
        if place >= 2:
            acc = attend(acc, distances[place - 2])
        own, acc = lax.optimization_barrier((arrived[distance], acc))
        arrived[distance] = own
        with jax.named_scope("along_head"):
            across = lax.ppermute(own, "head", swap)
        with jax.named_scope("along_inner"):
            visitors[distance] = (own, across, lax.ppermute(own, "inner", swap), lax.ppermute(across, "inner", swap))
    if count > 2:
        acc = attend(acc, distances[-2])

    flat = [part for distance in distances for part in visitors[distance]]
    attended, log_total = pl.pallas_call(
        functools.partial(last_kernel, coef, distances[-1], distances),
        in_specs=[scalars] + [whole] * 6 + [in_hbm] * 2 + [anywhere] * len(flat),
        out_specs=[pl.BlockSpec(query_rows.shape), pl.BlockSpec((2, heads, rows))],
        out_shape=[
            jax.ShapeDtypeStruct(query_rows.shape, query_rows.dtype),
            jax.ShapeDtypeStruct((2, heads, rows), jnp.float32),
        ],
        scratch_shapes=kv_buffers
        + [
            pltpu.VMEM((2, heads, rows, width), jnp.float32),
            pltpu.VMEM(acc_shape.shape, jnp.float32),
            pltpu.SemaphoreType.DMA,
        ],
        cost_estimate=cost(2, 7_000_000),
        compiler_params=params,
        name="last_visitor",
    )(slot_block, qx, acc, *visitors[distances[-1]], key_rows, value_rows, *flat)
    return attended, log_total


def solution(mesh):
    placed = (
        P(("groups", "seq"), "inner", "head"),
        P(("groups", "seq"), None, None),
        P(("groups", "seq"), None, None),
        P(),
    )
    return jax.shard_map(
        body,
        mesh=mesh,
        in_specs=placed,
        out_specs=(P(("groups", "seq"), "inner", "head"), P(("groups", "seq"), "head", "inner")),
        check_vma=False,
    )
```

time: 53.3 us -> 43 us (0.81)
  Pallas kernels: 23.3 us -> 16.7 us
  waiting for transfers between devices: 11.7 us -> 9.45 us
  starting transfers between devices: 12.3 us -> 11.2 us
    ppermute x3, waiting for transfers between devices: 6.64 us -> 1.73 us  [along_seq(): return lax.ppermute(block, 'seq', route)]
    pallas_call x3, Pallas kernels: 16.4 us -> 12 us  [the longest x2 6.02 us: attend(): pl.pallas_call(functools.partial(middle_kernel, coef, distance), in_specs...]
    ppermute x3, waiting for transfers between devices: 5.07 us -> 7.7 us  [body(): across = lax.ppermute(own, 'head', swap)]
    pallas_call x1, Pallas kernels: 6.91 us -> 4.66 us  [body(): pl.pallas_call(functools.partial(last_kernel, coef, distances[-1], distan...]
    ppermute x3, starting transfers between devices: 8.16 us -> 6.13 us  [along_seq(): return lax.ppermute(block, 'seq', route)]
    ppermute x3, starting transfers between devices: 3.64 us -> 4.55 us  [body(): across = lax.ppermute(own, 'head', swap)]
  transfers between devices with their start and end apart: 12 -> 12, of which waited for: 3 -> 3; matrix products, arithmetic and copies ran while one was open for 0% -> 0% of each run, Pallas kernels for 31% -> 28%
where the time goes in v3:
time: 43 us; the launch traced here: 43.1 us
  Pallas kernels  16.7 us (39%)
  starting transfers between devices  11.2 us (26%)
  waiting for transfers between devices  9.45 us (22%)
  local copies, waits for them, and re-layouts  3.69 us (9%)
  other arithmetic  1.19 us (3%)
  between operations  0.87 us (2%)
    ppermute x3, waiting for transfers between devices, body(): across = lax.ppermute(own, 'head', swap)  7.7 us
    ppermute x3, starting transfers between devices, along_seq(): return lax.ppermute(block, 'seq', route)  6.13 us
    pallas_call x2, Pallas kernels, attend(): pl.pallas_call(functools.partial(middle_kernel, coef, distance), in_specs...  6.02 us
    pallas_call x1, Pallas kernels, body(): pl.pallas_call(functools.partial(local_kernel, coef), in_specs=[scalars]...  5.99 us
    pallas_call x1, Pallas kernels, body(): pl.pallas_call(functools.partial(last_kernel, coef, distances[-1], distan...  4.66 us
    ppermute x3, starting transfers between devices, body(): across = lax.ppermute(own, 'head', swap)  4.55 us
    unnamed x8, local copies, waits for them, and re-layouts  3.69 us
    ppermute x3, waiting for transfers between devices, along_seq(): return lax.ppermute(block, 'seq', route)  1.73 us
  transfers between devices with their start and end apart: 12, of which 3 were waited for; matrix products, arithmetic and copies ran while one was open for 0% of the time, Pallas kernels for 28%

profile of v3, /device:TPU:0, one launch (start us, length us, event | category | flops | bytes accessed | tf_op | source)
XLA Modules:
  0.0 43.1 jit_solution(17702179038812991244)
XLA Ops:
  0.6 1.2 %select_bitcast_fusion = bf16[640,128]{1,0:T(8,128)(2,1)S(1)} fusion(bf16[2,640,128]{2,1,0:T(8,128)(2,1)} %rest_1_.1, bf16[2,640,128]{2,1,0:T(8,128)(2,1)} %rest_0_.1, pred[]{:T(512)S(6)} %eq.8, pred[]{:T(512)S(6)} %eq.7), kind=kLoop, calls=%fused_computation | loop fusion | flops 245760 | bytes 819202 | tf_op jit(solution)/shard_map/pieces/jit(_where)/select_n | solution.py:263
  1.8 4.1 %collective-permute-start.1 = (bf16[640,128]{1,0:T(8,128)(2,1)S(1)}, bf16[640,128]{1,0:T(8,128)(2,1)S(1)}, u32[]{:S(2)}, u32[]{:S(2)}) collective-permute-start(bf16[640,128]{1,0:T(8,128)(2,1)S(1)} %select_bitcast_fusion), channel_id=1, source_target_pairs={{0,8},{4,12},{8,0},{12,4},{1,9},{5,13},{9,1},{13,5},{2,10},{6,14},... | collective-permute-start | bytes 491528 | tf_op jit(solution)/shard_map/along_seq/ppermute | solution.py:256
  5.9 1.6 %collective-permute-start = (bf16[640,128]{1,0:T(8,128)(2,1)S(1)}, bf16[640,128]{1,0:T(8,128)(2,1)S(1)}, u32[]{:S(2)}, u32[]{:S(2)}) collective-permute-start(bf16[640,128]{1,0:T(8,128)(2,1)S(1)} %select_bitcast_fusion), channel_id=1, source_target_pairs={{0,4},{4,0},{8,12},{12,8},{1,5},{5,1},{9,13},{13,9},{2,6},{6,2},{1... | collective-permute-start | bytes 491528 | tf_op jit(solution)/shard_map/along_seq/ppermute | solution.py:256
  7.5 1.0 %copy-done = bf16[2,640,128]{2,1,0:T(8,128)(2,1)S(1)} copy-done((bf16[2,640,128]{2,1,0:T(8,128)(2,1)S(1)}, bf16[2,640,128]{2,1,0:T(8,128)(2,1)}, u32[]{:S(2)}) %copy-start) | copy-done | bytes 327704
  8.5 1.0 %copy-done.1 = bf16[2,640,128]{2,1,0:T(8,128)(2,1)S(1)} copy-done((bf16[2,640,128]{2,1,0:T(8,128)(2,1)S(1)}, bf16[2,640,128]{2,1,0:T(8,128)(2,1)}, u32[]{:S(2)}) %copy-start.1) | copy-done | bytes 327704
  9.5 0.7 %copy-done.2 = s32[8]{0:T(128)S(1)} copy-done((s32[8]{0:T(128)S(1)}, s32[8]{0:T(128)}, u32[]{:S(2)}) %copy-start.2) | copy-done | bytes 56
  10.1 1.1 %copy-done.3 = bf16[2,320,512]{2,1,0:T(8,128)(2,1)S(1)} copy-done((bf16[2,320,512]{2,1,0:T(8,128)(2,1)S(1)}, bf16[2,320,512]{2,1,0:T(8,128)(2,1)}, u32[]{:S(2)}) %copy-start.3) | copy-done | bytes 655384
  11.2 6.0 %local_part.1 = (bf16[2,4,320,256]{3,2,1,0:T(8,128)(2,1)S(1)}, f32[2,4,320,256]{3,2,1,0:T(8,128)S(1)}) custom-call(s32[8]{0:T(128)S(1)} %copy-done.2, bf16[2,320,512]{2,1,0:T(8,128)(2,1)S(1)} %copy-done.3, bf16[2,640,128]{2,1,0:T(8,128)(2,1)S(1)} %copy-done, bf16[2,640,128]{2,1,0:T(8,128)(2,1)S(1)} %copy-done.1), custom_call_target="tpu_custom_call" | custom-call | flops 2516582400 | bytes 6000000 | tf_op jit(solution)/shard_map/local_part/pallas_call | solution.py:283
  17.2 0.0 collective-permute-done.1.p0.rest_6_
  17.2 0.0 collective-permute-done.p0.rest_2_
  17.2 1.6 %collective-permute-start.3 = (bf16[640,128]{1,0:T(8,128)(2,1)S(1)}, bf16[640,128]{1,0:T(8,128)(2,1)S(1)}, u32[]{:S(2)}, u32[]{:S(2)}) collective-permute-start(bf16[640,128]{1,0:T(8,128)(2,1)S(1)} %collective-permute-done.p0.rest_2_), channel_id=1, source_target_pairs={{0,2},{2,0},{1,3},{3,1},{4,6},{6,4},{5,7},{7,5},{8,10},{10,8},{9,1... | collective-permute-start | bytes 491528 | tf_op jit(solution)/shard_map/along_head/ppermute | solution.py:319
  18.8 0.0 collective-permute-start.4
  18.8 3.9 %collective-permute-done.3.p1.rest_3_ = bf16[640,128]{1,0:T(8,128)(2,1)S(1)} collective-permute-done((bf16[640,128]{1,0:T(8,128)(2,1)S(1)}, bf16[640,128]{1,0:T(8,128)(2,1)S(1)}, u32[]{:S(2)}, u32[]{:S(2)}) %collective-permute-start.3) | collective-permute-done | bytes 163872 | tf_op jit(solution)/shard_map/along_head/ppermute | solution.py:319
  22.7 0.0 collective-permute-start.5
  22.7 0.4 %collective-permute-start.2 = (bf16[640,128]{1,0:T(8,128)(2,1)S(1)}, bf16[640,128]{1,0:T(8,128)(2,1)S(1)}, u32[]{:S(2)}, u32[]{:S(2)}) collective-permute-start(bf16[640,128]{1,0:T(8,128)(2,1)S(1)} %collective-permute-done.1.p0.rest_6_), channel_id=1, source_target_pairs={{0,4},{4,0},{8,12},{12,8},{1,5},{5,1},{9,13},{13,9},{2,6},{6,2},{1... | collective-permute-start | bytes 491528 | tf_op jit(solution)/shard_map/along_seq/ppermute | solution.py:256
  23.1 1.5 %collective-permute-start.6 = (bf16[640,128]{1,0:T(8,128)(2,1)S(1)}, bf16[640,128]{1,0:T(8,128)(2,1)S(1)}, u32[]{:S(2)}, u32[]{:S(2)}) collective-permute-start(bf16[640,128]{1,0:T(8,128)(2,1)S(1)} %collective-permute-done.1.p0.rest_6_), channel_id=1, source_target_pairs={{0,2},{2,0},{1,3},{3,1},{4,6},{6,4},{5,7},{7,5},{8,10},{10,8},{9,1... | collective-permute-start | bytes 491528 | tf_op jit(solution)/shard_map/along_head/ppermute | solution.py:319
  24.6 0.0 collective-permute-done.4.p2.rest_4_
  24.6 0.0 collective-permute-done.5.p3.rest_5_
  24.6 2.9 %visitor_1.1.acc_in = f32[2,4,320,256]{3,2,1,0:T(8,128)S(1)} custom-call(s32[8]{0:T(128)S(1)} %copy-done.2, bf16[2,4,320,256]{3,2,1,0:T(8,128)(2,1)S(1)} %get-tuple-element.13.qx_ref, f32[2,4,320,256]{3,2,1,0:T(8,128)S(1)} %get-tuple-element.20.acc_in, bf16[640,128]{1,0:T(8,128)(2,1)S(1)} %collective-permute-done.p0.rest_2_, ...), custom_call_target="tpu_custom_call", output_to_operand_aliasing={{}: (2, {})} | custom-call | flops 1677721600 | bytes 7000000 | tf_op jit(solution)/shard_map/visitor_1/pallas_call | solution.py:295
  27.5 1.7 %collective-permute-done.2.p0.rest_10_ = bf16[640,128]{1,0:T(8,128)(2,1)S(1)} collective-permute-done((bf16[640,128]{1,0:T(8,128)(2,1)S(1)}, bf16[640,128]{1,0:T(8,128)(2,1)S(1)}, u32[]{:S(2)}, u32[]{:S(2)}) %collective-permute-start.2) | collective-permute-done | bytes 163872 | tf_op jit(solution)/shard_map/along_seq/ppermute | solution.py:256
  29.3 1.5 %collective-permute-start.9 = (bf16[640,128]{1,0:T(8,128)(2,1)S(1)}, bf16[640,128]{1,0:T(8,128)(2,1)S(1)}, u32[]{:S(2)}, u32[]{:S(2)}) collective-permute-start(bf16[640,128]{1,0:T(8,128)(2,1)S(1)} %collective-permute-done.2.p0.rest_10_), channel_id=1, source_target_pairs={{0,2},{2,0},{1,3},{3,1},{4,6},{6,4},{5,7},{7,5},{8,10},{10,8},{9,1... | collective-permute-start | bytes 491528 | tf_op jit(solution)/shard_map/along_head/ppermute | solution.py:319
  30.8 0.0 collective-permute-start.7
  30.8 0.0 collective-permute-done.6.p1.rest_7_
  30.8 0.5 %collective-permute-start.8 = (bf16[640,128]{1,0:T(8,128)(2,1)S(1)}, bf16[640,128]{1,0:T(8,128)(2,1)S(1)}, u32[]{:S(2)}, u32[]{:S(2)}) collective-permute-start(bf16[640,128]{1,0:T(8,128)(2,1)S(1)} %collective-permute-done.6.p1.rest_7_), channel_id=1, source_target_pairs={{0,1},{1,0},{2,3},{3,2},{4,5},{5,4},{6,7},{7,6},{8,9},{9,8},{10,11... | collective-permute-start | bytes 491528 | tf_op jit(solution)/shard_map/along_inner/ppermute | solution.py:321
  31.3 0.0 collective-permute-start.10
  31.3 3.8 %collective-permute-done.9.p1.rest_11_ = bf16[640,128]{1,0:T(8,128)(2,1)S(1)} collective-permute-done((bf16[640,128]{1,0:T(8,128)(2,1)S(1)}, bf16[640,128]{1,0:T(8,128)(2,1)S(1)}, u32[]{:S(2)}, u32[]{:S(2)}) %collective-permute-start.9) | collective-permute-done | bytes 163872 | tf_op jit(solution)/shard_map/along_head/ppermute | solution.py:319
  35.1 0.0 collective-permute-start.11
  35.1 0.0 collective-permute-done.7.p2.rest_8_
  35.1 0.0 collective-permute-done.8.p3.rest_9_
  35.1 3.1 %visitor_2.1.acc_ref = f32[2,4,320,256]{3,2,1,0:T(8,128)S(1)} custom-call(s32[8]{0:T(128)S(1)} %copy-done.2, bf16[2,4,320,256]{3,2,1,0:T(8,128)(2,1)S(1)} %get-tuple-element.13.qx_ref, f32[2,4,320,256]{3,2,1,0:T(8,128)S(1)} %visitor_1.1.acc_in, bf16[640,128]{1,0:T(8,128)(2,1)S(1)} %collective-permute-done.1.p0.rest_6_, ...), custom_call_target="tpu_custom_call", output_to_operand_aliasing={{}: (2, {})} | custom-call | flops 1677721600 | bytes 7000000 | tf_op jit(solution)/shard_map/visitor_2/pallas_call | solution.py:295
  38.2 0.0 collective-permute-done.10.p2.rest_12_
  38.2 4.7 %last_visitor.1 = (bf16[2,320,512]{2,1,0:T(8,128)(2,1)}, f32[2,4,320]{2,1,0:T(4,128)}) custom-call(s32[8]{0:T(128)S(1)} %copy-done.2, bf16[2,4,320,256]{3,2,1,0:T(8,128)(2,1)S(1)} %get-tuple-element.13.qx_ref, f32[2,4,320,256]{3,2,1,0:T(8,128)S(1)} %visitor_2.1.acc_ref, bf16[640,128]{1,0:T(8,128)(2,1)S(1)} %collective-permute-done.2.p0.rest_10_, ...), custom_call_target="tpu_custom_call" | custom-call | flops 1677721600 | bytes 7000000 | tf_op jit(solution)/shard_map/last_visitor/pallas_call | solution.py:326
  (5 shorter events, 0.0 us)
Async XLA Ops:
  1.8 15.4 %collective-permute-start.1 = (bf16[640,128]{1,0:T(8,128)(2,1)S(1)}, bf16[640,128]{1,0:T(8,128)(2,1)S(1)}, u32[]{:S(2)}, u32[]{:S(2)}) collective-permute-start(bf16[640,128]{1,0:T(8,128)(2,1)S(1)} %select_bitcast_fusion), channel_id=1, source_target_pairs={{0,8},{4,12},{8,0},{12,4},{1,9},{5,13},{9,1},{13,5},{2,10},{6,14},... | collective-permute-start | bytes 491528 | tf_op jit(solution)/shard_map/along_seq/ppermute | solution.py:256
  5.9 11.3 %collective-permute-start = (bf16[640,128]{1,0:T(8,128)(2,1)S(1)}, bf16[640,128]{1,0:T(8,128)(2,1)S(1)}, u32[]{:S(2)}, u32[]{:S(2)}) collective-permute-start(bf16[640,128]{1,0:T(8,128)(2,1)S(1)} %select_bitcast_fusion), channel_id=1, source_target_pairs={{0,4},{4,0},{8,12},{12,8},{1,5},{5,1},{9,13},{13,9},{2,6},{6,2},{1... | collective-permute-start | bytes 491528 | tf_op jit(solution)/shard_map/along_seq/ppermute | solution.py:256
  7.5 1.0 %copy-start = (bf16[2,640,128]{2,1,0:T(8,128)(2,1)S(1)}, bf16[2,640,128]{2,1,0:T(8,128)(2,1)}, u32[]{:S(2)}) copy-start(bf16[2,640,128]{2,1,0:T(8,128)(2,1)} %rest_0_.1) | copy-start | bytes 983044
  8.5 1.0 %copy-start.1 = (bf16[2,640,128]{2,1,0:T(8,128)(2,1)S(1)}, bf16[2,640,128]{2,1,0:T(8,128)(2,1)}, u32[]{:S(2)}) copy-start(bf16[2,640,128]{2,1,0:T(8,128)(2,1)} %rest_1_.1) | copy-start | bytes 983044
  9.5 0.7 %copy-start.2 = (s32[8]{0:T(128)S(1)}, s32[8]{0:T(128)}, u32[]{:S(2)}) copy-start(s32[8]{0:T(128)} %sb.7) | copy-start | bytes 100
  10.1 1.1 %copy-start.3 = (bf16[2,320,512]{2,1,0:T(8,128)(2,1)S(1)}, bf16[2,320,512]{2,1,0:T(8,128)(2,1)}, u32[]{:S(2)}) copy-start(bf16[2,320,512]{2,1,0:T(8,128)(2,1)} %q_hbm.1) | copy-start | bytes 1966084
  17.2 5.4 %collective-permute-start.3 = (bf16[640,128]{1,0:T(8,128)(2,1)S(1)}, bf16[640,128]{1,0:T(8,128)(2,1)S(1)}, u32[]{:S(2)}, u32[]{:S(2)}) collective-permute-start(bf16[640,128]{1,0:T(8,128)(2,1)S(1)} %collective-permute-done.p0.rest_2_), channel_id=1, source_target_pairs={{0,2},{2,0},{1,3},{3,1},{4,6},{6,4},{5,7},{7,5},{8,10},{10,8},{9,1... | collective-permute-start | bytes 491528 | tf_op jit(solution)/shard_map/along_head/ppermute | solution.py:319
  18.8 5.8 %collective-permute-start.4 = (bf16[640,128]{1,0:T(8,128)(2,1)S(1)}, bf16[640,128]{1,0:T(8,128)(2,1)S(1)}, u32[]{:S(2)}, u32[]{:S(2)}) collective-permute-start(bf16[640,128]{1,0:T(8,128)(2,1)S(1)} %collective-permute-done.p0.rest_2_), channel_id=1, source_target_pairs={{0,1},{1,0},{2,3},{3,2},{4,5},{5,4},{6,7},{7,6},{8,9},{9,8},{10,11... | collective-permute-start | bytes 491528 | tf_op jit(solution)/shard_map/along_inner/ppermute | solution.py:321
  22.7 2.0 %collective-permute-start.5 = (bf16[640,128]{1,0:T(8,128)(2,1)S(1)}, bf16[640,128]{1,0:T(8,128)(2,1)S(1)}, u32[]{:S(2)}, u32[]{:S(2)}) collective-permute-start(bf16[640,128]{1,0:T(8,128)(2,1)S(1)} %collective-permute-done.3.p1.rest_3_), channel_id=1, source_target_pairs={{0,1},{1,0},{2,3},{3,2},{4,5},{5,4},{6,7},{7,6},{8,9},{9,8},{10,11... | collective-permute-start | bytes 491528 | tf_op jit(solution)/shard_map/along_inner/ppermute | solution.py:321
  22.7 6.6 %collective-permute-start.2 = (bf16[640,128]{1,0:T(8,128)(2,1)S(1)}, bf16[640,128]{1,0:T(8,128)(2,1)S(1)}, u32[]{:S(2)}, u32[]{:S(2)}) collective-permute-start(bf16[640,128]{1,0:T(8,128)(2,1)S(1)} %collective-permute-done.1.p0.rest_6_), channel_id=1, source_target_pairs={{0,4},{4,0},{8,12},{12,8},{1,5},{5,1},{9,13},{13,9},{2,6},{6,2},{1... | collective-permute-start | bytes 491528 | tf_op jit(solution)/shard_map/along_seq/ppermute | solution.py:256
  23.1 7.7 %collective-permute-start.6 = (bf16[640,128]{1,0:T(8,128)(2,1)S(1)}, bf16[640,128]{1,0:T(8,128)(2,1)S(1)}, u32[]{:S(2)}, u32[]{:S(2)}) collective-permute-start(bf16[640,128]{1,0:T(8,128)(2,1)S(1)} %collective-permute-done.1.p0.rest_6_), channel_id=1, source_target_pairs={{0,2},{2,0},{1,3},{3,1},{4,6},{6,4},{5,7},{7,5},{8,10},{10,8},{9,1... | collective-permute-start | bytes 491528 | tf_op jit(solution)/shard_map/along_head/ppermute | solution.py:319
  29.3 5.8 %collective-permute-start.9 = (bf16[640,128]{1,0:T(8,128)(2,1)S(1)}, bf16[640,128]{1,0:T(8,128)(2,1)S(1)}, u32[]{:S(2)}, u32[]{:S(2)}) collective-permute-start(bf16[640,128]{1,0:T(8,128)(2,1)S(1)} %collective-permute-done.2.p0.rest_10_), channel_id=1, source_target_pairs={{0,2},{2,0},{1,3},{3,1},{4,6},{6,4},{5,7},{7,5},{8,10},{10,8},{9,1... | collective-permute-start | bytes 491528 | tf_op jit(solution)/shard_map/along_head/ppermute | solution.py:319
  30.8 4.3 %collective-permute-start.7 = (bf16[640,128]{1,0:T(8,128)(2,1)S(1)}, bf16[640,128]{1,0:T(8,128)(2,1)S(1)}, u32[]{:S(2)}, u32[]{:S(2)}) collective-permute-start(bf16[640,128]{1,0:T(8,128)(2,1)S(1)} %collective-permute-done.1.p0.rest_6_), channel_id=1, source_target_pairs={{0,1},{1,0},{2,3},{3,2},{4,5},{5,4},{6,7},{7,6},{8,9},{9,8},{10,11... | collective-permute-start | bytes 491528 | tf_op jit(solution)/shard_map/along_inner/ppermute | solution.py:321
  30.8 4.3 %collective-permute-start.8 = (bf16[640,128]{1,0:T(8,128)(2,1)S(1)}, bf16[640,128]{1,0:T(8,128)(2,1)S(1)}, u32[]{:S(2)}, u32[]{:S(2)}) collective-permute-start(bf16[640,128]{1,0:T(8,128)(2,1)S(1)} %collective-permute-done.6.p1.rest_7_), channel_id=1, source_target_pairs={{0,1},{1,0},{2,3},{3,2},{4,5},{5,4},{6,7},{7,6},{8,9},{9,8},{10,11... | collective-permute-start | bytes 491528 | tf_op jit(solution)/shard_map/along_inner/ppermute | solution.py:321
  31.3 6.9 %collective-permute-start.10 = (bf16[640,128]{1,0:T(8,128)(2,1)S(1)}, bf16[640,128]{1,0:T(8,128)(2,1)S(1)}, u32[]{:S(2)}, u32[]{:S(2)}) collective-permute-start(bf16[640,128]{1,0:T(8,128)(2,1)S(1)} %collective-permute-done.2.p0.rest_10_), channel_id=1, source_target_pairs={{0,1},{1,0},{2,3},{3,2},{4,5},{5,4},{6,7},{7,6},{8,9},{9,8},{10,11... | collective-permute-start | bytes 491528 | tf_op jit(solution)/shard_map/along_inner/ppermute | solution.py:321
  35.1 3.1 %collective-permute-start.11 = (bf16[640,128]{1,0:T(8,128)(2,1)S(1)}, bf16[640,128]{1,0:T(8,128)(2,1)S(1)}, u32[]{:S(2)}, u32[]{:S(2)}) collective-permute-start(bf16[640,128]{1,0:T(8,128)(2,1)S(1)} %collective-permute-done.9.p1.rest_11_), channel_id=1, source_target_pairs={{0,1},{1,0},{2,3},{3,2},{4,5},{5,4},{6,7},{7,6},{8,9},{9,8},{10,11... | collective-permute-start | bytes 491528 | tf_op jit(solution)/shard_map/along_inner/ppermute | solution.py:321

commit v4 on v3

v4 whole, which is shorter than its diff:
```python
import functools
import math

import jax
import jax.numpy as jnp
from jax import lax
from jax.experimental import pallas as pl
from jax.experimental.pallas import tpu as pltpu
from jax.sharding import PartitionSpec as P

NEG = -1e30
SUM_LIMIT = 1e36
LO, HI = 0, 1


def score_dot(q, k):
    return lax.dot_general(q, k, (((1,), (1,)), ((), ())), preferred_element_type=jnp.float32)


def value_dot(p, v):
    return jnp.dot(p, v, preferred_element_type=jnp.float32)


def widen(x, width):
    return jnp.concatenate([x] * (width // x.shape[1]), axis=1)


def with_ones(x):
    return jnp.concatenate([x, jnp.ones_like(x)], axis=1)


def is_power(count):
    return count & (count - 1) == 0


def source_of(index, distance, count):
    if is_power(count):
        return index ^ distance
    return lax.rem(index - distance + count, count)


def blocks_of(sb, seq_index):
    b0, b1 = sb[2 * seq_index], sb[2 * seq_index + 1]
    return jnp.where(b1 > b0, 1, 0), jnp.minimum(b0, b1), jnp.maximum(b0, b1)


def minus_columns(top):
    high = top.astype(jnp.bfloat16)
    rest = top - high.astype(jnp.float32)
    middle = rest.astype(jnp.bfloat16)
    low = (rest - middle.astype(jnp.float32)).astype(jnp.bfloat16)
    lane = lax.broadcasted_iota(jnp.int32, top.shape, 1)
    high, middle, low = (x.astype(jnp.float32) for x in (high, middle, low))
    picked = jnp.where(lane == 0, high, jnp.where(lane == 1, middle, jnp.where(lane == 2, low, 0.0)))
    return (-picked).astype(jnp.bfloat16)


def local_heads(coef, inner, q_buf, k_buf, v_buf, qx_ref, acc_ref, first, ready_values):
    heads = qx_ref.shape[1]
    _, block_len, width = k_buf.shape
    rows = q_buf.shape[1]
    row = lax.broadcasted_iota(jnp.int32, (rows, block_len), 0) + inner * rows
    col = lax.broadcasted_iota(jnp.int32, (rows, block_len), 1)
    causal = col <= row

    def lanes_max(s):
        return jnp.broadcast_to(jnp.max(s, axis=1, keepdims=True), (rows, width))

    def weights(s, top):
        return jnp.exp2((s - widen(top, block_len)) * coef).astype(jnp.bfloat16)

    def scores(h):
        q_lo = q_buf[LO, :, (first + h) * width : (first + h + 1) * width]
        q_hi = q_buf[HI, :, (first + h) * width : (first + h + 1) * width]
        past = score_dot(q_hi, k_buf[LO])
        diag = jnp.where(causal, score_dot(q_hi, k_buf[HI]), NEG)
        low = jnp.where(causal, score_dot(q_lo, k_buf[LO]), NEG)
        return q_lo, q_hi, past, diag, low

    ready = scores(0)
    ready_values()
    for h in range(heads):
        q_lo, q_hi, past, diag, low = ready
        if h + 1 < heads:
            ready = scores(h + 1)
        v_lo, v_hi = with_ones(v_buf[LO]), with_ones(v_buf[HI])
        top = lanes_max(jnp.maximum(past, diag))
        acc_ref[HI, h] = value_dot(weights(past, top), v_lo) + value_dot(weights(diag, top), v_hi)
        qx_ref[HI, h] = jnp.concatenate([q_hi, minus_columns(top)], axis=1)
        top = lanes_max(low)
        acc_ref[LO, h] = value_dot(weights(low, top), v_lo)
        qx_ref[LO, h] = jnp.concatenate([q_lo, minus_columns(top)], axis=1)


def local_first(coef, sb, q_hbm, k_hbm, v_hbm, qx_ref, acc_ref, q_buf, k_buf, v_buf, sems):
    hi, _, _ = blocks_of(sb, lax.axis_index("seq"))
    copies = []
    for place, (src, dst) in enumerate([(k_hbm, k_buf), (q_hbm, q_buf), (v_hbm, v_buf)]):
        for order, slot in ((LO, 1 - hi), (HI, hi)):
            copies.append(pltpu.make_async_copy(src.at[slot], dst.at[order], sems.at[place, order]))
    for copy in copies:
        copy.start()
    for copy in copies[:4]:
        copy.wait()

    def ready_values():
        for copy in copies[4:]:
            copy.wait()

    local_heads(coef, lax.axis_index("inner"), q_buf, k_buf, v_buf, qx_ref, acc_ref, 0, ready_values)


def local_second(coef, first, q_buf, k_buf, v_buf, qx_ref, acc_ref):
    local_heads(coef, lax.axis_index("inner"), q_buf, k_buf, v_buf, qx_ref, acc_ref, first, lambda: None)


def head_places(parts):
    return [(part, h) for part in parts for h in range(part.shape[1])]


def visit(coef, distance, sb, qx, acc, parts, k_buf, v_buf, store):
    places = head_places(qx)
    heads = len(places)
    _, block_len, width = k_buf.shape
    count = lax.axis_size("seq")
    me = lax.axis_index("seq")
    head_index = lax.rem(lax.axis_index("head"), 2)
    inner = lax.axis_index("inner")
    for value, (own_buf, twin_buf) in enumerate([(k_buf, v_buf), (v_buf, k_buf)]):

        @pl.when(inner == value)
        def _():
            for turn in range(2):
                slot = head_index if turn == 0 else 1 - head_index
                own_buf[slot] = parts[turn][...]
                twin_buf[slot] = parts[2 + turn][...]

    _, _, top_block = blocks_of(sb, me)
    other_hi, _, other_top = blocks_of(sb, source_of(me, distance, count))
    other_lo = 1 - other_hi
    above = top_block > other_top

    def weights(s):
        return jnp.exp2(s * coef).astype(jnp.bfloat16)

    def in_turn(chunks, score, finish):
        ready = score(*chunks[0])
        for place, chunk in enumerate(chunks):
            now = ready
            if place + 1 < len(chunks):
                ready = score(*chunks[place + 1])
            finish(weights(now), *chunk)

    @pl.when(above)
    def _():
        def score(h):
            keys = with_ones(k_buf[...].reshape(2 * block_len, width))
            return score_dot(places[h][0][HI, places[h][1]], keys)

        def finish(p, h):
            values = with_ones(v_buf[...].reshape(2 * block_len, width))
            store(HI, h, acc[h][0][HI, acc[h][1]] + value_dot(p, values))
            store(LO, h, None)

        in_turn([(h,) for h in range(heads)], score, finish)

    @pl.when(jnp.logical_not(above))
    def _():
        def score(h, order):
            return score_dot(places[h][0][order, places[h][1]], with_ones(k_buf[other_lo]))

        def finish(p, h, order):
            store(order, h, acc[h][0][order, acc[h][1]] + value_dot(p, with_ones(v_buf[other_lo])))

        in_turn([(h, order) for h in range(heads) for order in (HI, LO)], score, finish)


def first_row(x):
    return jnp.transpose(x)[:1]


def middle_kernel(coef, distance, n, sb, *refs):
    qx, pieces, outs = refs[:n], refs[2 * n : 2 * n + 4], refs[2 * n + 4 : 3 * n + 4]
    *tops, k_buf, v_buf = refs[3 * n + 4 :]
    acc = head_places(outs)
    width = k_buf.shape[2]

    def store(order, h, value):
        if value is not None:
            acc[h][0][order, acc[h][1]] = value

    visit(coef, distance, sb, qx, acc, pieces, k_buf, v_buf, store)
    for top_ref in tops:
        for order in (LO, HI):
            for h, (part, place) in enumerate(head_places(qx)):
                columns = jnp.transpose(part[order, place, :, width:].astype(jnp.float32))
                top_ref[order, h : h + 1, :] = -(columns[0:1] + columns[1:2] + columns[2:3])


def last_kernel(coef, distance, distances, n, sb, *refs):
    qx, acc, top_ref, pieces = refs[:n], head_places(refs[n : 2 * n]), refs[2 * n], refs[2 * n + 1 : 2 * n + 5]
    every, rest = refs[2 * n + 5 :][: 4 * len(distances) + 2], refs[2 * n + 5 :][4 * len(distances) + 2 :]
    out_hbm, lse_ref, out_buf, k_buf, v_buf, worst, run_top, run_acc, sem, out_sems = rest
    heads = len(acc)
    rows = worst.shape[0]
    _, block_len, width = k_buf.shape
    count = lax.axis_size("seq")
    me = lax.axis_index("seq")
    head_index = lax.rem(lax.axis_index("head"), 2)
    inner = lax.axis_index("inner")
    hi, lo_block, hi_block = blocks_of(sb, me)

    def out_copy(h):
        columns = pl.ds(h * width, width)
        return pltpu.make_async_copy(out_buf.at[:, :, columns], out_hbm.at[:, :, columns], out_sems.at[h])

    def emit(order, h, value, top_row):
        slot = hi if order == HI else 1 - hi
        sums = value[:, width:]
        out_buf[slot, :, h * width : (h + 1) * width] = (value[:, :width] / sums).astype(out_buf.dtype)
        lse_ref[slot, h : h + 1, :] = top_row * (coef * math.log(2.0)) + jnp.log(first_row(sums))
        return sums

    worst[...] = jnp.zeros_like(worst)

    def store(order, h, value):
        if value is None:
            value = acc[h][0][order, acc[h][1]]
        sums = emit(order, h, value, top_ref[order, h : h + 1, :])
        worst[...] = jnp.maximum(worst[...], sums)
        if order == LO:
            out_copy(h).start()

    visit(coef, distance, sb, qx, acc, pieces, k_buf, v_buf, store)
    for h in range(heads):
        out_copy(h).wait()

    @pl.when(jnp.logical_not(jnp.max(worst[...]) < SUM_LIMIT))
    def _():
        def fetch(src, buf, slot):
            copy = pltpu.make_async_copy(src, buf.at[slot], sem)
            copy.start()
            copy.wait()

        def online(source):
            base = 0
            for part in qx:

                @pl.loop(0, 4 * part.shape[1])
                def _(i):
                    h, slot, order = i // 4, lax.rem(i, 4) // 2, lax.rem(i, 2)
                    own_block = jnp.where(order == HI, hi_block, lo_block)
                    shift = (own_block - sb[2 * source + slot]) * block_len + inner * rows

                    @pl.when(shift + rows > 0)
                    def _():
                        s = score_dot(part[order, h, :, :width], k_buf[slot])
                        row = lax.broadcasted_iota(jnp.int32, s.shape, 0) + shift
                        allowed = lax.broadcasted_iota(jnp.int32, s.shape, 1) <= row
                        s = jnp.where(allowed, s, NEG)
                        before = run_top[order, base + h]
                        top = jnp.maximum(before, jnp.broadcast_to(jnp.max(s, axis=1, keepdims=True), before.shape))
                        p = jnp.where(allowed, jnp.exp2((s - widen(top, block_len)) * coef), 0.0)
                        run_top[order, base + h] = top
                        shrink = widen(jnp.exp2((before - top) * coef), 2 * width)
                        fresh = value_dot(p.astype(jnp.bfloat16), with_ones(v_buf[slot]))
                        run_acc[order, base + h] = run_acc[order, base + h] * shrink + fresh

                base += part.shape[1]

        run_top[...] = jnp.full_like(run_top, NEG)
        run_acc[...] = jnp.zeros_like(run_acc)
        for slot in range(2):
            fetch(every[0].at[slot], k_buf, slot)
            fetch(every[1].at[slot], v_buf, slot)
        online(me)
        for place, other in enumerate(distances):
            others = every[2 + 4 * place : 6 + 4 * place]
            for value, (own_buf, twin_buf) in enumerate([(k_buf, v_buf), (v_buf, k_buf)]):

                @pl.when(inner == value)
                def _():
                    for turn in range(2):
                        slot = head_index if turn == 0 else 1 - head_index
                        fetch(others[turn], own_buf, slot)
                        fetch(others[2 + turn], twin_buf, slot)

            online(source_of(me, other, count))
        for h in range(heads):
            for order in (LO, HI):
                emit(order, h, run_acc[order, h], first_row(run_top[order, h]))
            out_copy(h).start()
            out_copy(h).wait()


def body(query_rows, key_rows, value_rows, slot_block):
    _, block_len, width = key_rows.shape
    _, rows, feats = query_rows.shape
    heads = feats // width
    sizes = [heads] if heads == 1 else [heads // 2, heads - heads // 2]
    count = lax.axis_size("seq")
    coef = math.log2(math.e) / math.sqrt(width)
    distances = list(range(1, count))

    def along_seq(block, distance):
        if is_power(count):
            route = [(i, i ^ distance) for i in range(count)]
        else:
            route = [(i, (i + distance) % count) for i in range(count)]
        with jax.named_scope("along_seq"):
            return lax.ppermute(block, "seq", route)

    def along_head(block):
        with jax.named_scope("along_head"):
            return lax.ppermute(block, "head", [(i, i ^ 1) for i in range(lax.axis_size("head"))])

    def along_inner(block):
        with jax.named_scope("along_inner"):
            return lax.ppermute(block, "inner", [(0, 1), (1, 0)])

    head_index, inner_index = lax.rem(lax.axis_index("head"), 2), lax.axis_index("inner")
    with jax.named_scope("pieces"):
        held = [
            jnp.where(inner_index == 0, key_rows[slot], value_rows[slot]) for slot in range(2)
        ]
        piece = jnp.where(head_index == 0, held[0], held[1])
    arrived = {}
    for distance in distances:
        if not is_power(count) or is_power(distance):
            arrived[distance] = along_seq(piece, distance)

    whole = pl.BlockSpec(memory_space=pltpu.VMEM)
    anywhere = pl.BlockSpec(memory_space=pl.ANY)
    scalars = pl.BlockSpec(memory_space=pltpu.SMEM)
    acc_shapes = [jax.ShapeDtypeStruct((2, size, rows, 2 * width), jnp.float32) for size in sizes]
    qx_shapes = [jax.ShapeDtypeStruct(shape.shape, jnp.bfloat16) for shape in acc_shapes]
    top_shape = jax.ShapeDtypeStruct((2, heads, rows), jnp.float32)
    params = pltpu.CompilerParams(vmem_limit_bytes=40 * 1024 * 1024)
    unit = rows * heads * block_len * width * 4
    exps = rows * heads * block_len

    def cost(units, size):
        return pl.CostEstimate(flops=int(2 * units * unit), bytes_accessed=size, transcendentals=int(units * exps))

    query_rows, key_rows, value_rows, slot_hbm = (
        pltpu.with_memory_space_constraint(x, pltpu.HBM) for x in (query_rows, key_rows, value_rows, slot_block)
    )
    kv_shape = jax.ShapeDtypeStruct(key_rows.shape, key_rows.dtype)
    qx0, acc0, q_sorted, k_sorted, v_sorted = pl.pallas_call(
        functools.partial(local_first, coef),
        in_specs=[scalars] + [anywhere] * 3,
        out_specs=[whole] * 5,
        out_shape=[qx_shapes[0], acc_shapes[0], jax.ShapeDtypeStruct(query_rows.shape, query_rows.dtype), kv_shape, kv_shape],
        scratch_shapes=[pltpu.SemaphoreType.DMA((3, 2))],
        cost_estimate=cost(1.5, 4_000_000),
        compiler_params=params,
        name="local_first",
    )(slot_hbm, query_rows, key_rows, value_rows)

    kv_buffers = [pltpu.VMEM((2, block_len, width), jnp.bfloat16)] * 2
    across, beside, beside_across = {}, {}, {}

    arrived[1], q_sorted = lax.optimization_barrier((arrived[1], q_sorted))
    across[1] = along_head(arrived[1])
    qx, acc = [qx0], [acc0]
    for size, qx_shape, acc_shape in zip(sizes[1:], qx_shapes[1:], acc_shapes[1:]):
        more_qx, more_acc = pl.pallas_call(
            functools.partial(local_second, coef, heads - size),
            in_specs=[whole] * 3,
            out_specs=[whole] * 2,
            out_shape=[qx_shape, acc_shape],
            cost_estimate=cost(1.5, 4_000_000),
            compiler_params=params,
            name="local_second",
        )(q_sorted, k_sorted, v_sorted)
        qx.append(more_qx)
        acc.append(more_acc)
    n = len(sizes)

    def attend(acc, distance, with_tops):
        return pl.pallas_call(
            functools.partial(middle_kernel, coef, distance, n),
            in_specs=[scalars] + [whole] * (2 * n + 4),
            out_specs=[whole] * (n + with_tops),
            out_shape=acc_shapes + [top_shape] * with_tops,
            scratch_shapes=kv_buffers,
            input_output_aliases={1 + n + i: i for i in range(n)},
            cost_estimate=cost(2, 7_000_000),
            compiler_params=params,
            name=f"visitor_{distance}",
        )(slot_block, *qx, *acc, arrived[distance], across[distance], beside[distance], beside_across[distance])

    for place, distance in enumerate(distances):
        following = distances[place + 1] if place + 1 < len(distances) else None
        tied = (acc, across[distance], arrived.get(following))
        acc, across[distance], ahead = lax.optimization_barrier(tied)
        if following is None:
            beside[distance] = along_inner(arrived[distance])
            beside_across[distance] = along_inner(across[distance])
            break
        arrived[following] = ahead
        after = distances[place + 2] if place + 2 < len(distances) else None
        if after is not None and after not in arrived:
            near = after & -after
            arrived[after] = along_seq(arrived[after ^ near], near)
        across[following] = along_head(arrived[following])
        beside[distance] = along_inner(arrived[distance])
        beside_across[distance] = along_inner(across[distance])
        found = attend(acc, distance, int(after is None))
        acc, tops = found[:n], found[n:]

    last = distances[-1]
    flat = [part for d in distances for part in (arrived[d], across[d], beside[d], beside_across[d])]
    attended, log_total = pl.pallas_call(
        functools.partial(last_kernel, coef, last, distances, n),
        in_specs=[scalars] + [whole] * (2 * n + 5) + [anywhere] * (2 + len(flat)),
        out_specs=[anywhere, pl.BlockSpec(top_shape.shape)],
        out_shape=[jax.ShapeDtypeStruct(query_rows.shape, query_rows.dtype), top_shape],
        scratch_shapes=[pltpu.VMEM(query_rows.shape, query_rows.dtype)]
        + kv_buffers
        + [
            pltpu.VMEM((rows, width), jnp.float32),
            pltpu.VMEM((2, heads, rows, width), jnp.float32),
            pltpu.VMEM((2, heads, rows, 2 * width), jnp.float32),
            pltpu.SemaphoreType.DMA,
            pltpu.SemaphoreType.DMA((heads,)),
        ],
        cost_estimate=cost(2, 7_000_000),
        compiler_params=params,
        name="last_visitor",
    )(slot_block, *qx, *acc, *tops, *flat[-4:], key_rows, value_rows, *flat)
    return attended, log_total


def solution(mesh):
    placed = (
        P(("groups", "seq"), "inner", "head"),
        P(("groups", "seq"), None, None),
        P(("groups", "seq"), None, None),
        P(),
    )
    return jax.shard_map(
        body,
        mesh=mesh,
        in_specs=placed,
        out_specs=(P(("groups", "seq"), "inner", "head"), P(("groups", "seq"), "head", "inner")),
        check_vma=False,
    )
```

time: 43 us -> 36.9 us (0.86)
  local copies, waits for them, and re-layouts: 3.69 us -> 0.01 us
  waiting for transfers between devices: 9.45 us -> 7.15 us
  Pallas kernels: 16.7 us -> 15.9 us
    unnamed x8 -> x2, local copies, waits for them, and re-layouts: 3.69 us -> 0.01 us
    ppermute x9, waiting for transfers between devices: 7.72 us -> 4.51 us  [the longest x3 3.11 us: along_head(): lax.ppermute(block, 'head', [(i, i ^ 1) for i in range(lax.axis_size('hea...]
    ppermute x3, waiting for transfers between devices: 1.73 us -> 2.64 us  [along_seq(): return lax.ppermute(block, 'seq', route)]
    pallas_call x4 -> x5, Pallas kernels: 16.7 us -> 15.9 us  [the longest x2 5.46 us: attend(): pl.pallas_call(functools.partial(middle_kernel, coef, distance, n), in_sp...]
    ppermute x9, starting transfers between devices: 5.07 us -> 5.82 us  [the longest x3 5.35 us: along_head(): lax.ppermute(block, 'head', [(i, i ^ 1) for i in range(lax.axis_size('hea...]
    ppermute x3, starting transfers between devices: 6.13 us -> 5.68 us  [along_seq(): return lax.ppermute(block, 'seq', route)]
  transfers between devices with their start and end apart: 12 -> 12, of which waited for: 3 -> 6; matrix products, arithmetic and copies ran while one was open for 0% -> 0% of each run, Pallas kernels for 28% -> 32%
where the time goes in v4:
time: 36.9 us; the launch traced here: 36.6 us
  Pallas kernels  15.9 us (43%)
  starting transfers between devices  11.5 us (31%)
  waiting for transfers between devices  7.15 us (19%)
  other arithmetic  1.19 us (3%)
  between operations  0.85 us (2%)
    ppermute x3, starting transfers between devices, along_seq(): return lax.ppermute(block, 'seq', route)  5.68 us
    pallas_call x2, Pallas kernels, attend(): pl.pallas_call(functools.partial(middle_kernel, coef, distance, n), in_sp...  5.46 us
    ppermute x3, starting transfers between devices, along_head(): lax.ppermute(block, 'head', [(i, i ^ 1) for i in range(lax.axis_size('hea...  5.35 us
    pallas_call x1, Pallas kernels, body(): pl.pallas_call(functools.partial(local_first, coef), in_specs=[scalars] +...  4.25 us
    pallas_call x1, Pallas kernels, body(): pl.pallas_call(functools.partial(last_kernel, coef, last, distances, n),...  4.07 us
    ppermute x3, waiting for transfers between devices, along_head(): lax.ppermute(block, 'head', [(i, i ^ 1) for i in range(lax.axis_size('hea...  3.11 us
    ppermute x3, waiting for transfers between devices, along_seq(): return lax.ppermute(block, 'seq', route)  2.64 us
    pallas_call x1, Pallas kernels, body(): pl.pallas_call(functools.partial(local_second, coef, heads - size), in_sp...  2.15 us
  transfers between devices with their start and end apart: 12, of which 6 were waited for; matrix products, arithmetic and copies ran while one was open for 0% of the time, Pallas kernels for 32%

profile of v4, /device:TPU:0, one launch (start us, length us, event | category | flops | bytes accessed | tf_op | source)
XLA Modules:
  0.0 36.6 jit_solution(16432792658945697432)
XLA Ops:
  0.6 1.2 %select_bitcast_fusion = bf16[640,128]{1,0:T(8,128)(2,1)S(1)} fusion(bf16[2,640,128]{2,1,0:T(8,128)(2,1)} %refs_10_.1, bf16[2,640,128]{2,1,0:T(8,128)(2,1)} %refs_9_.1, pred[]{:T(512)S(6)} %eq.8, pred[]{:T(512)S(6)} %eq.7), kind=kLoop, calls=%fused_computation | loop fusion | flops 245760 | bytes 819202 | tf_op jit(solution)/shard_map/pieces/jit(_where)/select_n | solution.py:326
  1.8 3.1 %collective-permute-start = (bf16[640,128]{1,0:T(8,128)(2,1)S(1)}, bf16[640,128]{1,0:T(8,128)(2,1)S(1)}, u32[]{:S(2)}, u32[]{:S(2)}) collective-permute-start(bf16[640,128]{1,0:T(8,128)(2,1)S(1)} %select_bitcast_fusion), channel_id=1, source_target_pairs={{0,4},{4,0},{8,12},{12,8},{1,5},{5,1},{9,13},{13,9},{2,6},{6,2},{1... | collective-permute-start | bytes 491528 | tf_op jit(solution)/shard_map/along_seq/ppermute | solution.py:311
  4.9 2.6 %collective-permute-start.2 = (bf16[640,128]{1,0:T(8,128)(2,1)S(1)}, bf16[640,128]{1,0:T(8,128)(2,1)S(1)}, u32[]{:S(2)}, u32[]{:S(2)}) collective-permute-start(bf16[640,128]{1,0:T(8,128)(2,1)S(1)} %select_bitcast_fusion), channel_id=1, source_target_pairs={{0,8},{4,12},{8,0},{12,4},{1,9},{5,13},{9,1},{13,5},{2,10},{6,14},... | collective-permute-start | bytes 491528 | tf_op jit(solution)/shard_map/along_seq/ppermute | solution.py:311
  7.5 4.2 %local_first.1 = (bf16[2,2,320,256]{3,2,1,0:T(8,128)(2,1)S(1)}, f32[2,2,320,256]{3,2,1,0:T(8,128)S(1)}, bf16[2,320,512]{2,1,0:T(8,128)(2,1)S(1)}, bf16[2,640,128...) custom-call(s32[8]{0:T(128)} %sb.7, bf16[2,320,512]{2,1,0:T(8,128)(2,1)} %q_hbm.1, bf16[2,640,128]{2,1,0:T(8,128)(2,1)} %refs_9_.1, ...), custom_call_target="tpu_custom_call" | custom-call | flops 1258291200 | bytes 4000000 | tf_op jit(solution)/shard_map/local_first/pallas_call | solution.py:349
  11.8 0.6 %collective-permute-done.refs_4_.refs_11_ = bf16[640,128]{1,0:T(8,128)(2,1)S(1)} collective-permute-done((bf16[640,128]{1,0:T(8,128)(2,1)S(1)}, bf16[640,128]{1,0:T(8,128)(2,1)S(1)}, u32[]{:S(2)}, u32[]{:S(2)}) %collective-permute-start) | collective-permute-done | bytes 163872 | tf_op jit(solution)/shard_map/along_seq/ppermute | solution.py:311
  12.4 1.8 %collective-permute-start.1 = (bf16[640,128]{1,0:T(8,128)(2,1)S(1)}, bf16[640,128]{1,0:T(8,128)(2,1)S(1)}, u32[]{:S(2)}, u32[]{:S(2)}) collective-permute-start(bf16[640,128]{1,0:T(8,128)(2,1)S(1)} %collective-permute-done.refs_4_.refs_11_), channel_id=1, source_target_pairs={{0,2},{2,0},{1,3},{3,1},{4,6},{6,4},{5,7},{7,5},{8,10},{10,8},{9,1... | collective-permute-start | bytes 491528 | tf_op jit(solution)/shard_map/along_head/ppermute | solution.py:315
  14.2 0.0 collective-permute-start.3
  14.2 0.0 copy-start
  14.2 2.1 %local_second.1 = (bf16[2,2,320,256]{3,2,1,0:T(8,128)(2,1)S(1)}, f32[2,2,320,256]{3,2,1,0:T(8,128)S(1)}) custom-call(bf16[2,320,512]{2,1,0:T(8,128)(2,1)S(1)} %get-tuple-element.29.q_buf, bf16[2,640,128]{2,1,0:T(8,128)(2,1)S(1)} %get-tuple-element.30.k_buf, bf16[2,640,128]{2,1,0:T(8,128)(2,1)S(1)} %get-tuple-element.31.v_buf), custom_call_target="tpu_custom_call" | custom-call | flops 1258291200 | bytes 4000000 | tf_op jit(solution)/shard_map/local_second/pallas_call | solution.py:367
  16.3 0.0 collective-permute-done.2.refs_4_.refs_15_
  16.3 1.3 %collective-permute-done.1.refs_5_.refs_12_ = bf16[640,128]{1,0:T(8,128)(2,1)S(1)} collective-permute-done((bf16[640,128]{1,0:T(8,128)(2,1)S(1)}, bf16[640,128]{1,0:T(8,128)(2,1)S(1)}, u32[]{:S(2)}, u32[]{:S(2)}) %collective-permute-start.1) | collective-permute-done | bytes 163872 | tf_op jit(solution)/shard_map/along_head/ppermute | solution.py:315
  17.7 0.0 collective-permute-start.4
  17.7 0.0 collective-permute-start.6
  17.7 1.8 %collective-permute-start.5 = (bf16[640,128]{1,0:T(8,128)(2,1)S(1)}, bf16[640,128]{1,0:T(8,128)(2,1)S(1)}, u32[]{:S(2)}, u32[]{:S(2)}) collective-permute-start(bf16[640,128]{1,0:T(8,128)(2,1)S(1)} %collective-permute-done.2.refs_4_.refs_15_), channel_id=1, source_target_pairs={{0,2},{2,0},{1,3},{3,1},{4,6},{6,4},{5,7},{7,5},{8,10},{10,8},{9,1... | collective-permute-start | bytes 491528 | tf_op jit(solution)/shard_map/along_head/ppermute | solution.py:315
  19.5 0.2 collective-permute-start.7
  19.7 0.0 collective-permute-done.3.refs_6_.refs_13_
  19.7 0.0 collective-permute-done.4.refs_7_.refs_14_
  19.7 0.0 copy-done
  19.7 2.5 %visitor_1.1 = (f32[2,2,320,256]{3,2,1,0:T(8,128)S(1)}, f32[2,2,320,256]{3,2,1,0:T(8,128)S(1)}) custom-call(s32[8]{0:T(128)S(1)} %copy-done, bf16[2,2,320,256]{3,2,1,0:T(8,128)(2,1)S(1)} %get-tuple-element.27.refs_0_, bf16[2,2,320,256]{3,2,1,0:T(8,128)(2,1)S(1)} %get-tuple-element.32.refs_1_, ...), custom_call_target="tpu_custom_call", output_to_operand_aliasing={{0}: (3, {}), {1}: (4, {})} | custom-call | flops 1677721600 | bytes 7000000 | tf_op jit(solution)/shard_map/visitor_1/pallas_call | solution.py:381
  22.3 2.0 %collective-permute-done.6.refs_5_.refs_19_ = bf16[640,128]{1,0:T(8,128)(2,1)S(1)} collective-permute-done((bf16[640,128]{1,0:T(8,128)(2,1)S(1)}, bf16[640,128]{1,0:T(8,128)(2,1)S(1)}, u32[]{:S(2)}, u32[]{:S(2)}) %collective-permute-start.6) | collective-permute-done | bytes 163872 | tf_op jit(solution)/shard_map/along_seq/ppermute | solution.py:311
  24.3 0.1 collective-permute-done.5.refs_5_.refs_16_
  24.4 0.0 collective-permute-start.8
  24.4 1.7 %collective-permute-start.9 = (bf16[640,128]{1,0:T(8,128)(2,1)S(1)}, bf16[640,128]{1,0:T(8,128)(2,1)S(1)}, u32[]{:S(2)}, u32[]{:S(2)}) collective-permute-start(bf16[640,128]{1,0:T(8,128)(2,1)S(1)} %collective-permute-done.6.refs_5_.refs_19_), channel_id=1, source_target_pairs={{0,2},{2,0},{1,3},{3,1},{4,6},{6,4},{5,7},{7,5},{8,10},{10,8},{9,1... | collective-permute-start | bytes 491528 | tf_op jit(solution)/shard_map/along_head/ppermute | solution.py:315
  26.1 0.2 collective-permute-start.10
  26.3 0.0 collective-permute-done.7.refs_6_.refs_17_
  26.3 0.0 collective-permute-done.8.refs_7_.refs_18_
  26.3 2.9 %visitor_2.1 = (f32[2,2,320,256]{3,2,1,0:T(8,128)S(1)}, f32[2,2,320,256]{3,2,1,0:T(8,128)S(1)}, f32[2,4,320]{2,1,0:T(4,128)S(1)}) custom-call(s32[8]{0:T(128)S(1)} %copy-done, bf16[2,2,320,256]{3,2,1,0:T(8,128)(2,1)S(1)} %get-tuple-element.27.refs_0_, ...), custom_call_target="tpu_custom_call", output_to_operand_aliasing={{0}: (3, {}), {1}: (4, {})} | custom-call | flops 1677721600 | bytes 7000000 | tf_op jit(solution)/shard_map/visitor_2/pallas_call | solution.py:381
  29.3 1.7 %collective-permute-done.9.refs_6_.refs_20_ = bf16[640,128]{1,0:T(8,128)(2,1)S(1)} collective-permute-done((bf16[640,128]{1,0:T(8,128)(2,1)S(1)}, bf16[640,128]{1,0:T(8,128)(2,1)S(1)}, u32[]{:S(2)}, u32[]{:S(2)}) %collective-permute-start.9) | collective-permute-done | bytes 163872 | tf_op jit(solution)/shard_map/along_head/ppermute | solution.py:315
  31.0 0.0 collective-permute-start.11
  31.0 0.0 collective-permute-done.10.refs_7_.refs_21_
  31.0 1.4 %collective-permute-done.11.refs_8_.refs_22_ = bf16[640,128]{1,0:T(8,128)(2,1)S(1)} collective-permute-done((bf16[640,128]{1,0:T(8,128)(2,1)S(1)}, bf16[640,128]{1,0:T(8,128)(2,1)S(1)}, u32[]{:S(2)}, u32[]{:S(2)}) %collective-permute-start.11) | collective-permute-done | bytes 163872 | tf_op jit(solution)/shard_map/along_inner/ppermute | solution.py:319
  32.4 4.1 %last_visitor.1 = (bf16[2,320,512]{2,1,0:T(8,128)(2,1)}, f32[2,4,320]{2,1,0:T(4,128)}) custom-call(s32[8]{0:T(128)S(1)} %copy-done, bf16[2,2,320,256]{3,2,1,0:T(8,128)(2,1)S(1)} %get-tuple-element.27.refs_0_, bf16[2,2,320,256]{3,2,1,0:T(8,128)(2,1)S(1)} %get-tuple-element.32.refs_1_, f32[2,2,320,256]{3,2,1,0:T(8,128)S(1)} %get-tuple-element.48.refs_2_, ...), custom_call_target="tpu_custom_call" | custom-call | flops 1677721600 | bytes 7000000 | tf_op jit(solution)/shard_map/last_visitor/pallas_call | solution.py:414
Async XLA Ops:
  1.8 10.5 %collective-permute-start = (bf16[640,128]{1,0:T(8,128)(2,1)S(1)}, bf16[640,128]{1,0:T(8,128)(2,1)S(1)}, u32[]{:S(2)}, u32[]{:S(2)}) collective-permute-start(bf16[640,128]{1,0:T(8,128)(2,1)S(1)} %select_bitcast_fusion), channel_id=1, source_target_pairs={{0,4},{4,0},{8,12},{12,8},{1,5},{5,1},{9,13},{13,9},{2,6},{6,2},{1... | collective-permute-start | bytes 491528 | tf_op jit(solution)/shard_map/along_seq/ppermute | solution.py:311
  4.9 11.4 %collective-permute-start.2 = (bf16[640,128]{1,0:T(8,128)(2,1)S(1)}, bf16[640,128]{1,0:T(8,128)(2,1)S(1)}, u32[]{:S(2)}, u32[]{:S(2)}) collective-permute-start(bf16[640,128]{1,0:T(8,128)(2,1)S(1)} %select_bitcast_fusion), channel_id=1, source_target_pairs={{0,8},{4,12},{8,0},{12,4},{1,9},{5,13},{9,1},{13,5},{2,10},{6,14},... | collective-permute-start | bytes 491528 | tf_op jit(solution)/shard_map/along_seq/ppermute | solution.py:311
  12.4 5.3 %collective-permute-start.1 = (bf16[640,128]{1,0:T(8,128)(2,1)S(1)}, bf16[640,128]{1,0:T(8,128)(2,1)S(1)}, u32[]{:S(2)}, u32[]{:S(2)}) collective-permute-start(bf16[640,128]{1,0:T(8,128)(2,1)S(1)} %collective-permute-done.refs_4_.refs_11_), channel_id=1, source_target_pairs={{0,2},{2,0},{1,3},{3,1},{4,6},{6,4},{5,7},{7,5},{8,10},{10,8},{9,1... | collective-permute-start | bytes 491528 | tf_op jit(solution)/shard_map/along_head/ppermute | solution.py:315
  14.2 5.6 %collective-permute-start.3 = (bf16[640,128]{1,0:T(8,128)(2,1)S(1)}, bf16[640,128]{1,0:T(8,128)(2,1)S(1)}, u32[]{:S(2)}, u32[]{:S(2)}) collective-permute-start(bf16[640,128]{1,0:T(8,128)(2,1)S(1)} %collective-permute-done.refs_4_.refs_11_), channel_id=1, source_target_pairs={{0,1},{1,0},{2,3},{3,2},{4,5},{5,4},{6,7},{7,6},{8,9},{9,8},{10,11... | collective-permute-start | bytes 491528 | tf_op jit(solution)/shard_map/along_inner/ppermute | solution.py:319
  14.2 5.6 %copy-start = (s32[8]{0:T(128)S(1)}, s32[8]{0:T(128)}, u32[]{:S(2)}) copy-start(s32[8]{0:T(128)} %sb.7) | copy-start | bytes 100
  17.7 2.0 %collective-permute-start.4 = (bf16[640,128]{1,0:T(8,128)(2,1)S(1)}, bf16[640,128]{1,0:T(8,128)(2,1)S(1)}, u32[]{:S(2)}, u32[]{:S(2)}) collective-permute-start(bf16[640,128]{1,0:T(8,128)(2,1)S(1)} %collective-permute-done.1.refs_5_.refs_12_), channel_id=1, source_target_pairs={{0,1},{1,0},{2,3},{3,2},{4,5},{5,4},{6,7},{7,6},{8,9},{9,8},{10,11... | collective-permute-start | bytes 491528 | tf_op jit(solution)/shard_map/along_inner/ppermute | solution.py:319
  17.7 6.6 %collective-permute-start.6 = (bf16[640,128]{1,0:T(8,128)(2,1)S(1)}, bf16[640,128]{1,0:T(8,128)(2,1)S(1)}, u32[]{:S(2)}, u32[]{:S(2)}) collective-permute-start(bf16[640,128]{1,0:T(8,128)(2,1)S(1)} %collective-permute-done.2.refs_4_.refs_15_), channel_id=1, source_target_pairs={{0,4},{4,0},{8,12},{12,8},{1,5},{5,1},{9,13},{13,9},{2,6},{6,2},{1... | collective-permute-start | bytes 491528 | tf_op jit(solution)/shard_map/along_seq/ppermute | solution.py:311
  17.7 6.7 %collective-permute-start.5 = (bf16[640,128]{1,0:T(8,128)(2,1)S(1)}, bf16[640,128]{1,0:T(8,128)(2,1)S(1)}, u32[]{:S(2)}, u32[]{:S(2)}) collective-permute-start(bf16[640,128]{1,0:T(8,128)(2,1)S(1)} %collective-permute-done.2.refs_4_.refs_15_), channel_id=1, source_target_pairs={{0,2},{2,0},{1,3},{3,1},{4,6},{6,4},{5,7},{7,5},{8,10},{10,8},{9,1... | collective-permute-start | bytes 491528 | tf_op jit(solution)/shard_map/along_head/ppermute | solution.py:315
  19.5 6.8 %collective-permute-start.7 = (bf16[640,128]{1,0:T(8,128)(2,1)S(1)}, bf16[640,128]{1,0:T(8,128)(2,1)S(1)}, u32[]{:S(2)}, u32[]{:S(2)}) collective-permute-start(bf16[640,128]{1,0:T(8,128)(2,1)S(1)} %collective-permute-done.2.refs_4_.refs_15_), channel_id=1, source_target_pairs={{0,1},{1,0},{2,3},{3,2},{4,5},{5,4},{6,7},{7,6},{8,9},{9,8},{10,11... | collective-permute-start | bytes 491528 | tf_op jit(solution)/shard_map/along_inner/ppermute | solution.py:319
  24.4 2.0 %collective-permute-start.8 = (bf16[640,128]{1,0:T(8,128)(2,1)S(1)}, bf16[640,128]{1,0:T(8,128)(2,1)S(1)}, u32[]{:S(2)}, u32[]{:S(2)}) collective-permute-start(bf16[640,128]{1,0:T(8,128)(2,1)S(1)} %collective-permute-done.5.refs_5_.refs_16_), channel_id=1, source_target_pairs={{0,1},{1,0},{2,3},{3,2},{4,5},{5,4},{6,7},{7,6},{8,9},{9,8},{10,11... | collective-permute-start | bytes 491528 | tf_op jit(solution)/shard_map/along_inner/ppermute | solution.py:319
  24.4 6.6 %collective-permute-start.9 = (bf16[640,128]{1,0:T(8,128)(2,1)S(1)}, bf16[640,128]{1,0:T(8,128)(2,1)S(1)}, u32[]{:S(2)}, u32[]{:S(2)}) collective-permute-start(bf16[640,128]{1,0:T(8,128)(2,1)S(1)} %collective-permute-done.6.refs_5_.refs_19_), channel_id=1, source_target_pairs={{0,2},{2,0},{1,3},{3,1},{4,6},{6,4},{5,7},{7,5},{8,10},{10,8},{9,1... | collective-permute-start | bytes 491528 | tf_op jit(solution)/shard_map/along_head/ppermute | solution.py:315
  26.1 4.9 %collective-permute-start.10 = (bf16[640,128]{1,0:T(8,128)(2,1)S(1)}, bf16[640,128]{1,0:T(8,128)(2,1)S(1)}, u32[]{:S(2)}, u32[]{:S(2)}) collective-permute-start(bf16[640,128]{1,0:T(8,128)(2,1)S(1)} %collective-permute-done.6.refs_5_.refs_19_), channel_id=1, source_target_pairs={{0,1},{1,0},{2,3},{3,2},{4,5},{5,4},{6,7},{7,6},{8,9},{9,8},{10,11... | collective-permute-start | bytes 491528 | tf_op jit(solution)/shard_map/along_inner/ppermute | solution.py:319
  31.0 1.4 %collective-permute-start.11 = (bf16[640,128]{1,0:T(8,128)(2,1)S(1)}, bf16[640,128]{1,0:T(8,128)(2,1)S(1)}, u32[]{:S(2)}, u32[]{:S(2)}) collective-permute-start(bf16[640,128]{1,0:T(8,128)(2,1)S(1)} %collective-permute-done.9.refs_6_.refs_20_), channel_id=1, source_target_pairs={{0,1},{1,0},{2,3},{3,2},{4,5},{5,4},{6,7},{7,6},{8,9},{9,8},{10,11... | collective-permute-start | bytes 491528 | tf_op jit(solution)/shard_map/along_inner/ppermute | solution.py:319
